TPU v7x, 32 devices: a whole 2x2x4 slice. The times are simulated.
32 devices in a mesh: wide: 8 (over y, x, core), narrow: 4 (over z).
Axes of the slice: x: 2, y: 2, z: 4, core: 2. Of those that a mesh axis runs over, the one named last changes fastest.
Arguments:
- tokens: bfloat16 [32768, 768], P(('wide', 'narrow')), may hold values from -6 to 6
- doc_lengths: int32 [64, 4], P(('wide', 'narrow')), may hold values from 1 to 256, 512 in all within a row
- cotangent: bfloat16 [32768, 768], P(('wide', 'narrow')), may hold values from -6 to 6
- owners: int32 [12], replicated, may hold values from 0 to 3, as said below
- step_count: int32 [1], replicated, may hold values from 1 to 20
- master: float32 [768, 24, 768], P('wide', 'narrow')
- moment_one: float32 [768, 24, 768], P('wide', 'narrow')
- moment_two: float32 [768, 24, 768], P('wide', 'narrow'), as said below
- vectors: float32 [13, 768], replicated
- vector_one: float32 [13, 768], replicated
- vector_two: float32 [13, 768], replicated, as said below
Outputs:
- layer_out: bfloat16 [32768, 768], P(('wide', 'narrow'))
- input_grad: float32 [32768, 768], P(('wide', 'narrow'))
- grad_norm: float32 [], replicated
- block_grads: float32 [768, 24, 768], P('wide', 'narrow')
- new_master: float32 [768, 24, 768], P('wide', 'narrow')
- new_first: float32 [768, 24, 768], P('wide', 'narrow')
- new_second: float32 [768, 24, 768], P('wide', 'narrow')
- new_copies: bfloat16 [768, 24, 768], P('wide', 'narrow')
- vector_grads: float32 [13, 768], replicated
- new_vectors: float32 [13, 768], replicated
- vector_first: float32 [13, 768], replicated
- vector_second: float32 [13, 768], replicated
Inputs may be any that keep to these rules, and one draw needn't show every extreme that they name: `owners`: each index of narrow owns at most 6 of the 12 blocks, and one owns exactly 6. `doc_lengths`: each row sums to 512; its longest document has exactly 256 tokens. `moment_two`: Positive. `vector_two`: Positive.
All inputs are finite; a program needn't handle non-finite values.
Results may differ from a plain program's by a relative error of at most 0.0098.
Values may be sent and summed in bfloat16 or wider, within the bound.
No kernel may reach another device: no remote copies, remote signals or barrier semaphores. Data moves between devices by JAX's collectives and lax.ppermute only.
A program may use at most 256 MiB of HBM per device.

v0:
```python
from functools import partial

import jax
import jax.numpy as jnp
from jax import lax
from jax.experimental import pallas as pl
from jax.experimental.pallas import tpu as pltpu
from jax.sharding import PartitionSpec as P

D = 768
HEADS = 12
HEAD = 64
ROT = 16
FF = 3072
SPREAD = FF // D

norm_epsilon = 1e-05
beta_first = 0.5
beta_second = 0.5
adam_epsilon = 1e-08
learn_rate = 0.02
vector_rate = 0.1
weight_decay = 0.1
masked_fill = -1e30
rope_base = 10000.0
LOG2E = 1.4426950408889634

BF = jnp.bfloat16
F32 = jnp.float32
MB = 1 << 20
ANY = pl.BlockSpec(memory_space=pl.ANY)
HBM = pl.BlockSpec(memory_space=pltpu.HBM)
SMEM = pl.BlockSpec(memory_space=pltpu.SMEM)
VMEM = pl.BlockSpec(memory_space=pltpu.VMEM)


def dot(a, b):
    return lax.dot_general(a, b, (((1,), (0,)), ((), ())), preferred_element_type=F32)


def dot_nt(a, b):
    return lax.dot_general(a, b, (((1,), (1,)), ((), ())), preferred_element_type=F32)


def dot_tn(a, b):
    return lax.dot_general(a, b, (((0,), (0,)), ((), ())), preferred_element_type=F32)


def params(mib, flops=0, moved=0, **more):
    return dict(
        compiler_params=pltpu.CompilerParams(vmem_limit_bytes=int(mib * MB), **more),
        cost_estimate=pl.CostEstimate(
            flops=int(flops), bytes_accessed=int(moved), transcendentals=0
        ),
    )


class Order:
    deps = ()


def ordered(body, *, in_specs, out_specs, out_shape, scratch_shapes=(), **more):
    single = not isinstance(out_shape, (list, tuple))
    specs, shapes = ([out_specs], [out_shape]) if single else (list(out_specs), list(out_shape))
    deps, n_in, n_out = Order.deps, len(in_specs), len(shapes)

    def wrapped(*refs):
        rest = refs[n_in + len(deps) :]
        body(*refs[:n_in], *rest[:n_out], *rest[n_out + 1 :])
        rest[n_out][...] = jnp.zeros((8, 128), F32)

    mark = VMEM if more.get("grid") is None else pl.BlockSpec((8, 128), lambda *at: (0, 0))
    call = pl.pallas_call(
        wrapped,
        in_specs=[*in_specs, *[ANY] * len(deps)],
        out_specs=[*specs, mark],
        out_shape=[*shapes, jax.ShapeDtypeStruct((8, 128), F32)],
        scratch_shapes=list(scratch_shapes),
        **more,
    )

    def run(*args):
        *out, token = call(*args, *deps)
        Order.deps = (token,)
        return out[0] if single else out

    return run


class Group:
    def __init__(self, arrays, pieces):
        self.arrays = tuple(arrays)
        self.pieces = tuple(pieces)


def row_of(spec, rows, me):
    if spec[0] == "at":
        return spec[1]
    return pl.multiple_of((me ^ spec[1]) * rows, rows)


def weight_copies(group, refs, first, count, dst, sems, me):
    copies = []
    for n, (array, lead, rows, spec) in enumerate(group.pieces):
        src = refs[array].at[lead + (pl.ds(first, count),)]
        copies.append(
            pltpu.make_async_copy(src, dst.at[:, pl.ds(row_of(spec, rows, me), rows)], sems.at[n])
        )
    return copies


def grad_copies(plan, refs, first, count, src, sems, me):
    blocks = pl.ds(first, count)
    return [
        pltpu.make_async_copy(
            src.at[blocks, pl.ds(row_of(spec, rows, me), rows)], refs[array].at[lead + (blocks,)], sems.at[n]
        )
        for n, (array, lead, rows, spec) in enumerate(plan)
    ]


def norms_of(x):
    mean = jnp.mean(x, axis=-1, keepdims=True)
    centred = x - mean
    scale = lax.rsqrt(jnp.mean(centred * centred, axis=-1, keepdims=True) + norm_epsilon)
    return centred * scale, scale


def layer_norms(tokens, vectors, deps=()):
    rows = tokens.shape[0]
    tile = 256

    def body(x_ref, v_ref, *rest):
        one_ref, two_ref = rest[len(deps) :]
        xhat, _ = norms_of(x_ref[...].astype(F32))
        one_ref[...] = (xhat * v_ref[0:1] + v_ref[1:2]).astype(BF)
        two_ref[...] = (xhat * v_ref[2:3] + v_ref[3:4]).astype(BF)

    spec = pl.BlockSpec((tile, D), lambda t: (t, 0))
    return ordered(
        body,
        grid=(rows // tile,),
        in_specs=[spec, pl.BlockSpec(vectors.shape, lambda t: (0, 0))] + [ANY] * len(deps),
        out_specs=[spec, spec],
        out_shape=[jax.ShapeDtypeStruct((rows, D), BF)] * 2,
        **params(16, 20 * rows * D, 6 * rows * D),
    )(tokens, vectors, *deps)


def pack_owned(here, owners, masters, blocks):
    rows = masters.shape[1]
    nb = len(blocks)

    def body(h_ref, o_ref, m_ref, out, stage, sems):
        copies, mine = [], []
        for i, b in enumerate(blocks):
            owner = o_ref[b]
            slot = jnp.int32(0)
            for before in range(b):
                slot = slot + (o_ref[before] == owner).astype(jnp.int32)
            mine.append(owner == h_ref[0])
            copies.append(pltpu.make_async_copy(m_ref.at[slot], stage.at[i], sems.at[i]))
            copies[-1].start()
        for i in range(nb):
            copies[i].wait()
            out[i] = jnp.where(mine[i], stage[i], 0.0).astype(BF)

    return ordered(
        body,
        in_specs=[SMEM, SMEM, ANY],
        out_specs=VMEM,
        out_shape=jax.ShapeDtypeStruct((nb, rows, D), BF),
        scratch_shapes=[pltpu.VMEM((nb, rows, D), F32), pltpu.SemaphoreType.DMA((nb,))],
        **params(16, 1, 1),
    )(here, owners, masters)


def gelu_pair(z):
    size = jnp.abs(z)
    t = pl.reciprocal(1.0 + (0.3275911 * 0.7071067811865476) * size)
    bell = jnp.exp2((-0.5 * LOG2E) * (z * z))
    poly = 0.5 * 1.061405429
    for c in (-1.453152027, 1.421413741, -0.284496736, 0.254829592):
        poly = poly * t + 0.5 * c
    tail = poly * t * bell
    cdf = jnp.where(z >= 0.0, 1.0 - tail, tail)
    return z * cdf, cdf + z * (bell * 0.3989422804014327)


def mlp_chunk(me, h_two, cot, bias, group, first, outs, plan, deps=()):
    rows = h_two.shape[0]
    part = 256
    parts = rows // part
    na, no, nd = len(group.arrays), len(outs), len(deps)
    n_in, n_out = len(group.pieces), len(plan)

    def body(me_ref, h_ref, y_ref, b_ref, *rest):
        w_refs, rest = rest[:na], rest[na + nd :]
        act_ref, dz_ref, db_ref = rest[:3]
        o_refs = rest[3 : 3 + no]
        h, y, w, act, dz, low, in_sem, t_sem, out_sem = rest[3 + no :]
        me_id = me_ref[0]
        at = [pl.ds(p * part, part) for p in range(parts)]
        loads = weight_copies(group, w_refs, first, 2, w, in_sem, me_id)
        tokens = [
            [
                pltpu.make_async_copy(src.at[at[p]], dst.at[at[p]], t_sem.at[n, p])
                for n, (src, dst) in enumerate(((h_ref, h), (y_ref, y)))
            ]
            for p in range(parts)
        ]
        for c in loads:
            c.start()
        for pair in tokens:
            for c in pair:
                c.start()
        for c in loads:
            c.wait()
        for pair in tokens:
            for c in pair:
                c.wait()
        stores, z, u, sums = [], {}, {}, []

        def into(p):
            z[p] = dot(h[at[p]], w[0]) + b_ref[...]
            u[p] = dot_nt(y[at[p]], w[1])

        def slopes(p):
            value, slope = gelu_pair(z[p])
            act[at[p]] = value.astype(BF)
            low_dz = (u[p] * slope).astype(BF)
            dz[at[p]] = low_dz
            sums.append(jnp.sum(low_dz.astype(F32), axis=0, keepdims=True))
            for n, (src, dst) in enumerate(((act, act_ref), (dz, dz_ref))):
                stores.append(pltpu.make_async_copy(src.at[at[p]], dst.at[at[p]], t_sem.at[2 + n, p]))
                stores[-1].start()

        for turn in range(parts + 1):
            if turn < parts:
                into(turn)
            if turn:
                slopes(turn - 1)
        for i, (left, right) in enumerate(((h, dz), (act, y))):
            low[i] = dot_tn(left[...], right[...]).astype(BF)
        for c in grad_copies(plan, o_refs, 0, 2, low, out_sem, me_id):
            c.start()
            stores.append(c)
        db_ref[...] = sum(sums[1:], sums[0])
        for c in stores:
            c.wait()

    act, dz, db, *grads = ordered(
        body,
        in_specs=[SMEM, HBM, HBM, VMEM] + [HBM] * na + [ANY] * nd,
        out_specs=[HBM, HBM, VMEM] + [HBM] * no,
        out_shape=[
            jax.ShapeDtypeStruct((rows, D), BF),
            jax.ShapeDtypeStruct((rows, D), BF),
            jax.ShapeDtypeStruct((1, D), F32),
            *outs,
        ],
        scratch_shapes=[
            pltpu.VMEM((rows, D), BF),
            pltpu.VMEM((rows, D), BF),
            pltpu.VMEM((2, D, D), BF),
            pltpu.VMEM((rows, D), BF),
            pltpu.VMEM((rows, D), BF),
            pltpu.VMEM((2, D, D), BF),
            pltpu.SemaphoreType.DMA((n_in,)),
            pltpu.SemaphoreType.DMA((4, parts)),
            pltpu.SemaphoreType.DMA((n_out,)),
        ],
        **params(60, 8 * rows * D * D, 16 * rows * D),
    )(me, h_two, cot, bias, *group.arrays, *deps)
    return act, dz, db, grads


def turned(x, cosine, from_right, from_left):
    return (
        x * cosine
        + pltpu.roll(x, 128 - ROT // 2, 1) * from_right
        + pltpu.roll(x, ROT // 2, 1) * from_left
    )


def lanes_of(cosine, sine):
    half = ROT // 2
    lane = lax.broadcasted_iota(jnp.int32, (half, 128), 1) % HEAD
    row = lax.broadcasted_iota(jnp.int32, (half, 128), 0)
    one, two = (lane == row).astype(F32), (lane == row + half).astype(F32)

    def spread(values, mask):
        return lax.dot_general(
            values, mask, (((0,), (0,)), ((), ())), precision=lax.Precision.HIGHEST, preferred_element_type=F32
        )

    still = (lax.broadcasted_iota(jnp.int32, (1, 128), 1) % HEAD >= ROT).astype(F32)
    return spread(cosine, one + two) + still, spread(sine, one), spread(sine, two)


def project(me, h_one, cot, bias, cosine, sine, group, deps=()):
    rows = h_one.shape[0]
    tile = 256
    per = cosine.shape[2] // tile
    na, n_in = len(group.arrays), len(group.pieces)

    def body(me_ref, h_ref, y_ref, b_ref, c_ref, s_ref, *rest):
        w_refs, rest = rest[:na], rest[na + len(deps) :]
        outs = rest[:4]
        w_all, sems = rest[4:]
        step = pl.program_id(0)

        @pl.when(step == 0)
        def _():
            copies = weight_copies(group, w_refs, 0, 4, w_all, sems, me_ref[0])
            for c in copies:
                c.start()
            for c in copies:
                c.wait()

        cos_l, right, left = lanes_of(c_ref[0], s_ref[0])
        outs[3][...] = dot_nt(y_ref[...], w_all[3]).astype(BF)
        for i in range(3):
            value = dot(h_ref[...], w_all[i]) + b_ref[i : i + 1]
            if i == 2:
                outs[2][...] = value.astype(BF)
                continue
            for j in range(D // 128):
                outs[i][:, j * 128 : (j + 1) * 128] = turned(
                    value[:, j * 128 : (j + 1) * 128], cos_l, -right, left
                ).astype(BF)

    spec = pl.BlockSpec((tile, D), lambda t: (t, 0))
    table = pl.BlockSpec((1, ROT // 2, tile), lambda t: (t // per, 0, t % per))
    return ordered(
        body,
        grid=(rows // tile,),
        in_specs=[SMEM, spec, spec, pl.BlockSpec((3, D), lambda t: (0, 0)), table, table]
        + [HBM] * na
        + [ANY] * len(deps),
        out_specs=[spec] * 4,
        out_shape=[jax.ShapeDtypeStruct((rows, D), BF)] * 4,
        scratch_shapes=[pltpu.VMEM((4, D, D), BF), pltpu.SemaphoreType.DMA((n_in,))],
        **params(60, 8 * rows * D * D, 20 * rows * D),
    )(me, h_one, cot, bias, cosine, sine, *group.arrays, *deps)


def attention(q, k, v, da, starts, cosine, sine, length, which, into=(), deps=()):
    rows = q.shape[0]
    seqs = len(which)
    half = length // 2
    pair = 128

    def body(q_ref, k_ref, v_ref, d_ref, st_ref, hc_ref, hs_ref, *rest):
        a_ref, dq_ref, dk_ref, dv_ref, db_ref, mask, wheel = rest[len(into) + len(deps) :]

        @pl.when(pl.program_id(1) == 0)
        def _():
            key = lax.broadcasted_iota(jnp.int32, (length, length), 0)
            query = lax.broadcasted_iota(jnp.int32, (length, length), 1)
            seen = (key <= query) & (key >= st_ref[0])
            mask[...] = jnp.where(seen, 0.0, masked_fill)
            wheel[0], wheel[1], wheel[2] = lanes_of(hc_ref[0], hs_ref[0])

        q_all, k_all, v_all, d_all = q_ref[...], k_ref[...], v_ref[...], d_ref[...]
        vt, kt = v_all.T, k_all.T
        dt = d_all.T.astype(F32)
        lane = lax.broadcasted_iota(jnp.int32, (length, pair), 1)
        zero = jnp.zeros((), BF)
        dv = [jnp.zeros((half, pair), F32)] * 2
        dk = [jnp.zeros((half, pair), F32)] * 2
        jobs = []
        for h in range(2):
            mine = (lane >= h * HEAD) & (lane < (h + 1) * HEAD)
            qm = jnp.where(mine, q_all, zero)
            dm = jnp.where(mine, d_all, zero)
            for b in range(2):
                jobs.append((h, b, qm[b * half : (b + 1) * half], dm[b * half : (b + 1) * half]))
        raw, dp, prob, low, at, ds, dqt = {}, {}, {}, {}, {}, {}, {}

        def scores(i):
            h, b, qm, dm = jobs[i]
            n = half * (b + 1)
            raw[i] = dot_nt(k_all[:n], qm)
            dp[i] = dot_nt(v_all[:n], dm)

        def softmax(i):
            h, b, qm, dm = jobs[i]
            n = half * (b + 1)
            s = raw[i] * (HEAD**-0.5 * LOG2E) + mask[:n, b * half : (b + 1) * half]
            e = jnp.exp2(s - jnp.max(s, axis=0, keepdims=True))
            prob[i] = e * (1.0 / jnp.sum(e, axis=0, keepdims=True))
            low[i] = prob[i].astype(BF)
            at[i] = dot(vt[h * HEAD : (h + 1) * HEAD, :n], low[i])

        def slopes(i):
            h, b, qm, dm = jobs[i]
            dh = dt[h * HEAD : (h + 1) * HEAD, b * half : (b + 1) * half]
            total = jnp.sum(dh * at[i], axis=0, keepdims=True)
            ds[i] = (prob[i] * (dp[i] - total)).astype(BF)

        def grads(i):
            h, b, qm, dm = jobs[i]
            n = half * (b + 1)
            dqt[i] = dot(kt[h * HEAD : (h + 1) * HEAD, :n], ds[i])
            more_v, more_k = dot(low[i], dm), dot(ds[i], qm)
            for c in range(b + 1):
                dv[c] = dv[c] + more_v[c * half : (c + 1) * half]
                dk[c] = dk[c] + more_k[c * half : (c + 1) * half]

        stages = (scores, softmax, slopes, grads)
        for turn in range(len(jobs) + len(stages) - 1):
            for n, stage in reversed(list(enumerate(stages))):
                if 0 <= turn - n < len(jobs):
                    stage(turn - n)
        at_h, dq_h = [], []
        for h in range(2):
            at_h.append(jnp.concatenate([at[2 * h], at[2 * h + 1]], axis=1))
            dq = jnp.concatenate([dqt[2 * h], dqt[2 * h + 1]], axis=1) * HEAD**-0.5
            u, w, cos, sin = dq[0:8], dq[8:16], hc_ref[0], hs_ref[0]
            dq_h.append(jnp.concatenate([u * cos + w * sin, w * cos - u * sin, dq[16:]], axis=0))
        a_ref[...] = jnp.concatenate(at_h, axis=0).astype(BF).T
        dq = jnp.concatenate(dq_h, axis=0).astype(BF).T
        dq_ref[...] = dq
        sums = [jnp.sum(dq.astype(F32), axis=0, keepdims=True)]
        sum_k = sum_v = jnp.zeros((1, pair), F32)
        for c in range(2):
            at_k = slice(c * half, (c + 1) * half)
            back = turned(dk[c] * HEAD**-0.5, wheel[0, at_k], wheel[1, at_k], -wheel[2, at_k]).astype(BF)
            dk_ref[at_k] = back
            sum_k = sum_k + jnp.sum(back.astype(F32), axis=0, keepdims=True)
            value = dv[c].astype(BF)
            dv_ref[at_k] = value
            sum_v = sum_v + jnp.sum(value.astype(F32), axis=0, keepdims=True)
        db_ref[0] = jnp.concatenate(sums + [sum_k, sum_v], axis=0)

    base = which[0]
    spec = pl.BlockSpec((length, pair), lambda s, h: (s + base, h))
    table = pl.BlockSpec((1, ROT // 2, length), lambda s, h: (s + base, 0, 0))
    a, dq, dk, dv, db = ordered(
        body,
        grid=(seqs, D // pair),
        in_specs=[spec] * 4
        + [pl.BlockSpec((1, 1, length), lambda s, h: (s + base, 0, 0)), table, table]
        + [ANY] * (len(into) + len(deps)),
        out_specs=[spec, spec, spec, spec, pl.BlockSpec((1, 3, pair), lambda s, h: (s, 0, h))],
        out_shape=[jax.ShapeDtypeStruct((rows, D), BF)] * 4
        + [jax.ShapeDtypeStruct((seqs, 3, D), F32)],
        scratch_shapes=[pltpu.VMEM((length, length), F32), pltpu.VMEM((3, length, 128), F32)],
        input_output_aliases={7 + n: n for n in range(len(into))},
        **params(60, 10e9 * seqs, 20 * rows * D),
    )(q, k, v, da, starts, cosine, sine, *into, *deps)
    return a, dq, dk, dv, db


def attention_grads(me, h_one, a, cot, dqkv, outs, plan, deps=()):
    rows = h_one.shape[0]
    no, n_out = len(outs), len(plan)

    def body(me_ref, h_ref, a_ref, y_ref, dq_ref, dk_ref, dv_ref, *rest):
        rest = rest[len(deps) :]
        o_refs = rest[:no]
        low, sems = rest[no:]
        pending = []
        for i, (left, right) in enumerate(
            ((h_ref, dq_ref), (h_ref, dk_ref), (h_ref, dv_ref), (a_ref, y_ref))
        ):
            low[i] = dot_tn(left[...], right[...]).astype(BF)
            if i % 2:
                copies = grad_copies(plan, o_refs, i - 1, 2, low, sems.at[i // 2], me_ref[0])
                for c in copies:
                    c.start()
                pending += copies
        for c in pending:
            c.wait()

    whole = pl.BlockSpec(memory_space=pltpu.VMEM)
    return ordered(
        body,
        in_specs=[SMEM] + [whole] * 6 + [ANY] * len(deps),
        out_specs=[HBM] * no,
        out_shape=list(outs),
        scratch_shapes=[pltpu.VMEM((4, D, D), BF), pltpu.SemaphoreType.DMA((2, n_out))],
        **params(60, 8 * rows * D * D, 12 * rows * D),
    )(me, h_one, a, cot, *dqkv, *deps)


def products(me, jobs, tail, outs, starts=None, extra=(), deps=(), mib=60):
    starts = starts or [()] * len(jobs)
    rows = jobs[0][0][0].shape[0]
    tile = 256
    groups, used = [], {}
    for job in jobs:
        for _, (group, i), _ in job:
            if id(group) not in used:
                groups.append(group)
                used[id(group)] = []
            used[id(group)].append(i)
    first, flat, runs, slot, at = {}, [], [], {}, 0
    for group in groups:
        first[id(group)] = len(flat)
        flat += list(group.arrays)
        low, high = min(used[id(group)]), max(used[id(group)])
        runs.append((group, low, high - low + 1, at))
        for i in range(low, high + 1):
            slot[id(group), i] = at
            at += 1
    lefts = [left for job in jobs for left, _, _ in job]
    begun = [x for group in starts for x in group]
    n_in = max(len(g.pieces) for g in groups)
    nl, ns, ne, nw, no = len(lefts), len(begun), len(extra), len(flat), len(outs)

    def body(me_ref, *rest):
        l_refs, rest = rest[:nl], rest[nl:]
        s_refs, rest = list(rest[:ns]), rest[ns:]
        e_refs, rest = rest[:ne], rest[ne:]
        w_refs, rest = rest[:nw], rest[nw + len(deps) :]
        o_refs, (w_all, sems) = rest[:no], rest[no:]
        step = pl.program_id(0)

        @pl.when(step == 0)
        def _():
            copies = []
            for n, (group, low, count, to) in enumerate(runs):
                refs = w_refs[first[id(group)] :]
                copies += weight_copies(
                    group, refs, low, count, w_all.at[pl.ds(to, count)], sems.at[n], me_ref[0]
                )
            for c in copies:
                c.start()
            for c in copies:
                c.wait()

        results, n = [], 0
        for job, begin in zip(jobs, starts):
            total = None
            for _ in begin:
                more = s_refs.pop(0)[...]
                total = more if total is None else total + more
            for _, (group, i), transposed in job:
                term = (dot_nt if transposed else dot)(l_refs[n][...], w_all[slot[id(group), i]])
                total = term if total is None else total + term
                n += 1
            results.append(total)
        tail(e_refs, results, o_refs, step)

    spec = pl.BlockSpec((tile, D), lambda t: (t, 0))

    def whole(x):
        return pl.BlockSpec(x.shape, lambda t: (0,) * len(x.shape))

    return ordered(
        body,
        grid=(rows // tile,),
        in_specs=[SMEM]
        + [spec] * (nl + ns)
        + [spec if per_token else whole(x) for x, per_token in extra]
        + [HBM] * nw
        + [ANY] * len(deps),
        out_specs=[spec if x.shape[0] == rows else whole(x) for x in outs],
        out_shape=list(outs),
        scratch_shapes=[pltpu.VMEM((at, D, D), BF), pltpu.SemaphoreType.DMA((len(runs), n_in))],
        **params(mib, 2 * nl * rows * D * D, (2 * nl + 8) * rows * D),
    )(me, *lefts, *begun, *[x for x, _ in extra], *flat, *deps)


def store_all(e_refs, results, o_refs, step):
    for ref, value in zip(o_refs, results):
        ref[...] = value


def add_rows(ref, terms, step):
    sums = jnp.concatenate([jnp.sum(term, axis=0, keepdims=True) for term in terms], axis=0)

    @pl.when(step == 0)
    def _():
        ref[...] = sums

    @pl.when(step > 0)
    def _():
        ref[...] += sums


def middle_tail(e_refs, results, o_refs, step):
    x_ref, y_ref, v_ref = e_refs
    out_ref, e_ref, sum_ref = o_refs
    out, d_one, d_two = results
    x = x_ref[...].astype(F32)
    out_ref[...] = out + x + (v_ref[7:8] + v_ref[8 + SPREAD : 9 + SPREAD])
    xhat, _ = norms_of(x)
    e_ref[...] = d_one * v_ref[0:1] + d_two * v_ref[2:3]
    add_rows(sum_ref, (d_one * xhat, d_one, d_two * xhat, d_two, y_ref[...].astype(F32)), step)


def last_tail(e_refs, results, o_refs, step):
    x_ref, y_ref, v_ref, e_ref = e_refs
    out_ref, grad_ref, sum_ref = o_refs
    out, d_two = results
    out_ref[...] = out.astype(BF)
    xhat, scale = norms_of(x_ref[...].astype(F32))
    e = e_ref[...] + d_two * v_ref[2:3]
    inner = jnp.mean(e * xhat, axis=-1, keepdims=True)
    y = y_ref[...].astype(F32)
    grad_ref[...] = y + (e - jnp.mean(e, axis=-1, keepdims=True) - xhat * inner) * scale
    add_rows(sum_ref, (d_two * xhat, d_two), step)


def adam(gradient, weight, moment, square, rate, decay, one_fix, two_fix):
    moment_new = beta_first * moment + (1.0 - beta_first) * gradient
    square_new = beta_second * square + (1.0 - beta_second) * gradient * gradient
    update = (moment_new * one_fix) / (jnp.sqrt(square_new * two_fix) + adam_epsilon)
    return weight - rate * (update + decay * weight), moment_new, square_new


def update_all(source, fixes, squares, vector_total, vector_state, summed, masters, firsts, seconds):
    slots, rows, _ = masters.shape
    ng = len(summed)

    def body(src_ref, fix_ref, q_ref, t_ref, vw_ref, vm_ref, vv_ref, *rest):
        g_refs, (w_ref, m_ref, v_ref) = rest[:ng], rest[ng : ng + 3]
        norm_out, tg_out, tw_out, tm_out, tv_out, g_out, w_out, m_out, v_out, c_out, clip_ref = rest[ng + 3 :]
        slot = pl.program_id(0)
        one_fix, two_fix = fix_ref[0], fix_ref[1]

        @pl.when(slot == 0)
        def _():
            t = t_ref[...]
            norm = jnp.sqrt(jnp.sum(q_ref[...], keepdims=True) + jnp.sum(t * t, keepdims=True))
            clip = jnp.minimum(1.0, 1.0 / (norm + 1e-06))
            norm_out[...] = norm
            clip_ref[...] = jnp.broadcast_to(clip, clip_ref.shape)
            gradient = t * clip
            new, moment, square = adam(
                gradient, vw_ref[...], vm_ref[...], vv_ref[...], vector_rate, 0.0, one_fix, two_fix
            )
            tg_out[...], tw_out[...], tm_out[...], tv_out[...] = gradient, new, moment, square

        keep = src_ref[2, slot] > 0
        low = g_refs[0][0]
        for n in range(1, ng):
            low = jnp.where(src_ref[0, slot] == n, g_refs[n][0], low)
        gradient = low.astype(F32) * clip_ref[0:1, 0:1]
        new, moment, square = adam(
            gradient, w_ref[0], m_ref[0], v_ref[0], learn_rate, weight_decay, one_fix, two_fix
        )
        new = jnp.where(keep, new, 0.0)
        g_out[0] = jnp.where(keep, gradient, 0.0)
        w_out[0] = new
        m_out[0] = jnp.where(keep, moment, 0.0)
        v_out[0] = jnp.where(keep, square, 0.0)
        c_out[0] = new.astype(BF)

    def whole(shape):
        return pl.BlockSpec(shape, lambda s, src, fix: (0,) * len(shape))

    def picked(n):
        return pl.BlockSpec(
            (1, rows, D), lambda s, src, fix: (jnp.where(src[0, s] == n, src[1, s], 0), 0, 0)
        )

    own = pl.BlockSpec((1, rows, D), lambda s, src, fix: (s, 0, 0))
    vec = vector_total.shape
    return pl.pallas_call(
        body,
        grid_spec=pltpu.PrefetchScalarGridSpec(
            num_scalar_prefetch=2,
            grid=(slots,),
            in_specs=[whole((8, 128))] + [whole(vec)] * 4 + [picked(n) for n in range(ng)] + [own] * 3,
            out_specs=[whole((1, 1))] + [whole(vec)] * 4 + [own] * 5,
            scratch_shapes=[pltpu.VMEM((8, 128), F32)],
        ),
        out_shape=[jax.ShapeDtypeStruct((1, 1), F32)]
        + [jax.ShapeDtypeStruct(vec, F32)] * 4
        + [jax.ShapeDtypeStruct((slots, rows, D), F32)] * 4
        + [jax.ShapeDtypeStruct((slots, rows, D), BF)],
        **params(24, 20 * slots * rows * D, 32 * slots * rows * D),
    )(source, fixes, squares, vector_total, *vector_state, *summed, masters, firsts, seconds)


def stacked(pieces, deps=()):
    count = len(pieces)

    def body(*refs):
        out, sems = refs[count + len(deps) :]
        copies = [pltpu.make_async_copy(refs[n], out.at[n], sems.at[n]) for n in range(count)]
        for c in copies:
            c.start()
        for c in copies:
            c.wait()

    return ordered(
        body,
        in_specs=[ANY] * (count + len(deps)),
        out_specs=VMEM,
        out_shape=jax.ShapeDtypeStruct((count, *pieces[0].shape), pieces[0].dtype),
        scratch_shapes=[pltpu.SemaphoreType.DMA((count,))],
        **params(16, 1, 1),
    )(*pieces, *deps)


def pair_sums(pairs, deps=()):
    chips, each, rows, _ = pairs[0][0].shape
    count = len(pairs)

    def body(*refs):
        outs = refs[2 * count + len(deps) :]
        for n in range(chips):

            @pl.when(pl.program_id(0) == n)
            def _(n=n):
                for i in range(count):
                    keep, got = refs[2 * i], refs[2 * i + 1]
                    outs[n][i * each : (i + 1) * each] = (keep[0].astype(F32) + got[0].astype(F32)).astype(BF)

    spec = pl.BlockSpec((1, each, rows, D), lambda n: (n, 0, 0, 0))
    one = (count * each, rows, D)
    return ordered(
        body,
        grid=(chips,),
        in_specs=[spec] * (2 * count) + [ANY] * len(deps),
        out_specs=[pl.BlockSpec(one, lambda n: (0, 0, 0))] * chips,
        out_shape=[jax.ShapeDtypeStruct(one, BF)] * chips,
        **params(16, 1, 1),
    )(*[x for pair in pairs for x in pair], *deps)


def total_of(*groups):
    flat = [x for group in groups for x in group]
    _, rows, _ = flat[0].shape
    blocks = sum(group[0].shape[0] for group in groups)

    def body(*refs):
        out, n, at = refs[len(flat)], 0, 0
        for group in groups:
            total = refs[n][...].astype(F32)
            for ref in refs[n + 1 : n + len(group)]:
                total = total + ref[...].astype(F32)
            out[at : at + total.shape[0]] = total.astype(BF)
            n, at = n + len(group), at + total.shape[0]

    return ordered(
        body,
        in_specs=[VMEM] * len(flat),
        out_specs=VMEM,
        out_shape=jax.ShapeDtypeStruct((blocks, rows, D), BF),
        **params(16, 1, 1),
    )(*flat)


def handed_on(value):
    def body(value_ref, out):
        pass

    return ordered(
        body,
        in_specs=[ANY],
        out_specs=ANY,
        out_shape=jax.ShapeDtypeStruct(value.shape, value.dtype),
        input_output_aliases={0: 0},
        **params(1, 1, 1),
    )(value)


def vector_terms(sums, last_sums, db_a, db_b, dbs):
    def body(s_ref, l_ref, a_ref, b_ref, *rest):
        out = rest[SPREAD]
        out[0:2] = s_ref[0:2]
        out[2:4] = s_ref[2:4] + l_ref[...]
        qkv = a_ref[0] + b_ref[0]
        for n in range(1, a_ref.shape[0]):
            qkv = qkv + (a_ref[n] + b_ref[n])
        out[4:7] = qkv
        out[7:8] = s_ref[4:5]
        for n in range(SPREAD):
            out[8 + n : 9 + n] = rest[n][...]
        out[8 + SPREAD : 9 + SPREAD] = s_ref[4:5]

    return ordered(
        body,
        in_specs=[VMEM] * (4 + SPREAD),
        out_specs=VMEM,
        out_shape=jax.ShapeDtypeStruct((9 + SPREAD, D), F32),
        **params(16, 1, 1),
    )(sums, last_sums, db_a, db_b, *dbs)


def plus(a, b):
    def body(a_ref, b_ref, out):
        out[...] = a_ref[...] + b_ref[...]

    return ordered(
        body,
        in_specs=[VMEM] * 2,
        out_specs=VMEM,
        out_shape=jax.ShapeDtypeStruct(a.shape, F32),
        **params(16, 1, 1),
    )(a, b)


def picked_end(here, value, outer):
    def body(h_ref, v_ref, o_ref, out):
        ends = (h_ref[0] == 0) | (h_ref[0] == 3)
        out[...] = jnp.where(ends, o_ref[...], v_ref[...])

    return ordered(
        body,
        in_specs=[SMEM, VMEM, VMEM],
        out_specs=VMEM,
        out_shape=jax.ShapeDtypeStruct(value.shape, BF),
        **params(16, 1, 1),
    )(here, value, outer)


def settled(here, value, outer):
    count, rows, _ = value.shape

    def body(h_ref, v_ref, o_ref, out_ref, q_ref):
        ends = (h_ref[0] == 0) | (h_ref[0] == 3)
        total = jnp.zeros((8, 128), F32)
        for n in range(count):
            kept = jnp.where(ends, o_ref[n], v_ref[n])
            out_ref[n] = kept
            x = kept.astype(F32)
            x = x * x
            for c in range(D // 128):
                part = x[:, c * 128 : (c + 1) * 128]
                for r in range(rows // 8):
                    total = total + part[r * 8 : (r + 1) * 8]
        q_ref[...] = total

    return ordered(
        body,
        in_specs=[SMEM, VMEM, VMEM],
        out_specs=[VMEM, VMEM],
        out_shape=[jax.ShapeDtypeStruct(value.shape, BF), jax.ShapeDtypeStruct((8, 128), F32)],
        **params(16, 1, 1),
    )(here, value, outer)


def swap(value, axis, bit):
    size = lax.axis_size(axis)
    return lax.ppermute(value, axis, [(i, i ^ bit) for i in range(size)])


CORE, SIDE, UP = 1, 2, 4
CHIPS = (0, SIDE, UP, SIDE | UP)


INWARD, ACROSS, OUTWARD = [(0, 1), (3, 2)], [(1, 2), (2, 1)], [(1, 0), (2, 3)]


def hop(value, pairs):
    if lax.axis_size("narrow") == 4:
        return lax.ppermute(value, "narrow", pairs)
    if pairs is INWARD:
        return (lax.psum(value.astype(F32), "narrow") - value.astype(F32)).astype(BF)
    return jnp.zeros_like(value) if pairs is ACROSS else value


def spread_wide(value):
    if lax.axis_size("wide") == 8:
        return [swap(value, "wide", m) for m in CHIPS[1:]]
    return None


def gather_wide(value):
    size = lax.axis_size("wide")
    count, rows, _ = value.shape
    full = lax.all_gather(value, "wide", axis=0, tiled=False)
    if rows % 16:
        full = jnp.swapaxes(full, 0, 1).reshape(1, count, D, D)
        size, rows = 1, D
    return Group((full,), [(0, (p,), rows, ("at", rows * p)) for p in range(size)])


def grad_layout(count, rows, size):
    if size != 8:
        return [jax.ShapeDtypeStruct((count, D, D), BF)], [(0, (), D, ("at", 0))]
    shape = jax.ShapeDtypeStruct((4, count, rows, D), BF)
    keep = [(0, (n,), rows, ("xor", m)) for n, m in enumerate(CHIPS)]
    give = [(1, (n,), rows, ("xor", m ^ CORE)) for n, m in enumerate(CHIPS)]
    return [shape] * 2, keep + give


def gathered(shard, parts):
    if parts is None:
        return gather_wide(shard)
    mine = stacked([shard, *parts])
    other = swap(mine, "wide", CORE)
    rows = shard.shape[1]
    masks = [(m, 0) for m in CHIPS] + [(m ^ CORE, 1) for m in CHIPS]
    return Group((mine, other), [(a, (n % 4,), rows, ("xor", m)) for n, (m, a) in enumerate(masks)])


def give(grads):
    if len(grads) == 1:
        return lax.psum_scatter(grads[0], "wide", scatter_dimension=1, tiled=True)
    return grads[0], swap(grads[1], "wide", CORE)


def exchange(*given):
    if not isinstance(given[0], tuple):
        return [given[0] if len(given) == 1 else jnp.concatenate(given, axis=0)]
    parts = pair_sums(list(given))
    return [parts[0]] + [swap(p, "wide", m) for p, m in zip(parts[1:], CHIPS[1:])]


def total_axis(value, axis):
    size = lax.axis_size(axis)
    bit = 1
    while bit < size:
        value = value + swap(value, axis, bit)
        bit *= 2
    return value


def slot_table(owners, capacity):
    number = owners.shape[0]
    order = jnp.arange(number, dtype=jnp.int32)
    before = (owners[:, None] == owners[None, :]) & (order[None, :] < order[:, None])
    return owners * capacity + jnp.sum(before.astype(jnp.int32), axis=1)


def per_device(tokens, doc_lengths, cotangent, owners, step_count, master, moment_one, moment_two, vectors, vector_one, vector_two):
    rows, capacity, _ = master.shape
    seqs = doc_lengths.shape[0]
    length = tokens.shape[0] // seqs
    blocks = owners.shape[0]
    wide = lax.axis_size("wide")
    narrow_index = lax.axis_index("narrow")
    me = lax.axis_index("wide").astype(jnp.int32).reshape(1)
    masters, firsts, seconds = [jnp.swapaxes(m, 0, 1) for m in (master, moment_one, moment_two)]

    here = narrow_index.astype(jnp.int32).reshape(1)
    local = slot_table(owners, capacity) - owners * capacity
    ends = jnp.cumsum(doc_lengths, axis=1)
    position = jnp.arange(length, dtype=jnp.int32)
    passed = position[None, None, :] >= ends[:, :, None]
    start = jnp.sum(jnp.where(passed, doc_lengths[:, :, None], 0), axis=1)
    freqs = jnp.power(rope_base, -2.0 * jnp.arange(ROT // 2, dtype=F32) / ROT)
    angle = (position[None] - start).astype(F32)[:, None, :] * freqs[None, :, None]
    cosine, sine = jnp.cos(angle), jnp.sin(angle)
    start = start[:, None, :]

    ids_0, ids_s, ids_t = (4, 8, 5, 9), (0, 1, 2, 3), (6, 10, 7, 11)
    pair_outs, pair_plan = grad_layout(2, rows, wide)
    four_outs, four_plan = grad_layout(4, rows, wide)
    full = jax.ShapeDtypeStruct(tokens.shape, F32)
    low = jax.ShapeDtypeStruct(tokens.shape, BF)
    acts, dzs, dbs, place = [], [], [], {}
    Order.deps = ()

    def arrived(group, ids):
        for i, b in enumerate(ids):
            place[b] = (group, i)

    def chunk(j):
        group, first = place[4 + j]
        act, dz, db, grads = mlp_chunk(
            me, h_two, cotangent, vectors[8 + j : 9 + j], group, first, pair_outs, pair_plan
        )
        acts.append(act)
        dzs.append(dz)
        dbs.append(db)
        return grads

    def forth(j):
        return (acts[j], place[8 + j], False)

    def back(j):
        return (dzs[j], place[4 + j], True)

    w_0 = pack_owned(here, owners, masters, ids_0)
    r_0 = hop(w_0, INWARD)
    h_one, h_two = layer_norms(tokens, vectors)
    w_0 = total_of([w_0, r_0])
    r_0 = hop(w_0, ACROSS)
    w_s = pack_owned(here, owners, masters, ids_s)
    r_s = hop(w_s, INWARD)
    w_0 = total_of([w_0, r_0])
    r_0 = hop(w_0, OUTWARD)
    w_s = total_of([w_s, r_s])
    r_s = hop(w_s, ACROSS)
    w_0 = picked_end(here, w_0, r_0)
    arrived(gather_wide(w_0), ids_0)
    w_t = pack_owned(here, owners, masters, ids_t)
    r_t = hop(w_t, INWARD)
    w_s = total_of([w_s, r_s])
    r_s = hop(w_s, OUTWARD)
    w_t = total_of([w_t, r_t])
    r_t = hop(w_t, ACROSS)
    w_s = picked_end(here, w_s, r_s)
    arrived(gather_wide(w_s), ids_s)
    w_t = total_of([w_t, r_t])
    r_t = hop(w_t, OUTWARD)
    s_0 = give(chunk(0))
    s_1 = give(chunk(1))
    w_t = picked_end(here, w_t, r_t)
    arrived(gather_wide(w_t), ids_t)
    front = exchange(s_0, s_1)
    q, k, v, da = project(me, h_one, cotangent, vectors[4:7], cosine, sine, place[0][0])
    half = seqs // 2
    *inner, db_a = attention(q, k, v, da, start, cosine, sine, length, tuple(range(half)))
    a, *dqkv, db_b = attention(
        q, k, v, da, start, cosine, sine, length, tuple(range(half, seqs)), into=inner
    )
    front = total_of(front)
    r_f = hop(front, INWARD)
    s_s = give(attention_grads(me, h_one, a, cotangent, dqkv, four_outs, four_plan))
    s_2 = give(chunk(2))
    front = total_of([front, r_f])
    r_f = hop(front, ACROSS)
    mid = exchange(s_s)
    middle, e_part, sums = products(
        me,
        [
            [(a, place[3], False), forth(2)],
            [(dqkv[n], place[n], True) for n in range(3)],
            [back(2)],
        ],
        middle_tail,
        [full, full, jax.ShapeDtypeStruct((5, D), F32)],
        extra=[(tokens, True), (cotangent, True), (vectors, False)],
    )
    front = total_of([front, r_f])
    r_f = hop(front, OUTWARD)
    third = exchange(s_2)
    mid = total_of(mid)
    r_m = hop(mid, INWARD)
    s_3 = chunk(3)
    mid = total_of([mid, r_m])
    r_m = hop(mid, ACROSS)
    third = total_of(third)
    r_h = hop(third, INWARD)
    last = exchange(give([*s_3[:-1], handed_on(s_3[-1])]))
    early = products(me, [[forth(0), forth(1)], [back(0), back(1)]], store_all, [full, full])
    last = total_of(last)
    r_l = hop(last, INWARD)
    mid = total_of([mid, r_m])
    r_m = hop(mid, OUTWARD)
    third = total_of([third, r_h])
    r_h = hop(third, ACROSS)
    layer_out, input_grad, last_sums = products(
        me,
        [[forth(3)], [back(3)]],
        last_tail,
        [low, full, jax.ShapeDtypeStruct((2, D), F32)],
        starts=[(middle, early[0]), (early[1],)],
        extra=[(tokens, True), (cotangent, True), (vectors, False), (e_part, True)],
    )
    vector_total = vector_terms(sums, last_sums, db_a, db_b, dbs)
    masks = [(axis, 1 << n) for axis in ("wide", "narrow") for n in range(lax.axis_size(axis).bit_length() - 1)]

    def vector_step(value):
        return plus(value, swap(value, *masks.pop(0)))

    last = total_of([last, r_l])
    r_l = hop(last, ACROSS)
    third = total_of([third, r_h])
    r_h = hop(third, OUTWARD)
    vector_total = vector_step(vector_total)
    vector_total = vector_step(vector_total)
    last = total_of([last, r_l])
    r_l = hop(last, OUTWARD)
    vector_total = vector_step(vector_total)
    front, front_square = settled(here, front, r_f)
    mid, mid_square = settled(here, mid, r_m)
    third, third_square = settled(here, third, r_h)
    while masks:
        vector_total = vector_step(vector_total)
    last, last_square = settled(here, last, r_l)
    squares = total_axis(front_square + mid_square + third_square + last_square, "wide")
    summed = (front, mid, third, last)
    held = ((4, 8, 5, 9), ids_s, (6, 10), (7, 11))
    step_float = step_count[0].astype(F32)
    fixes = jnp.stack(
        [1.0 / (1.0 - jnp.power(beta_first, step_float)), 1.0 / (1.0 - jnp.power(beta_second, step_float))]
    )
    slot = jnp.arange(capacity, dtype=jnp.int32)
    hit = ((owners == narrow_index)[None, :] & (local[None, :] == slot[:, None])).astype(jnp.int32)
    which, inner = [0] * blocks, [0] * blocks
    for n, ids in enumerate(held):
        for i, b in enumerate(ids):
            which[b], inner[b] = n, i
    source = jnp.stack(
        [
            jnp.sum(hit * jnp.array(which, jnp.int32)[None], axis=1),
            jnp.sum(hit * jnp.array(inner, jnp.int32)[None], axis=1),
            jnp.sum(hit, axis=1),
        ]
    )
    norm, vector_grads, new_vectors, vector_first, vector_second, *new = update_all(
        source, fixes, squares, vector_total, (vectors, vector_one, vector_two), summed, masters, firsts, seconds
    )
    block_grads, new_master, new_first, new_second, new_copies = [jnp.swapaxes(m, 0, 1) for m in new]
    return (
        layer_out,
        input_grad,
        norm[0, 0],
        block_grads,
        new_master,
        new_first,
        new_second,
        new_copies,
        vector_grads,
        new_vectors,
        vector_first,
        vector_second,
    )


def solution(mesh):
    tok = P(("wide", "narrow"), None)
    own = P("wide", "narrow", None)
    return jax.shard_map(
        per_device,
        mesh=mesh,
        in_specs=(tok, tok, tok, P(), P(), own, own, own, P(), P(), P()),
        out_specs=(tok, tok, P(), own, own, own, own, own, P(), P(), P(), P()),
        check_vma=False,
    )
```

profile of v0, /device:TPU:0, one launch (start us, length us, event | category | flops | bytes accessed | tf_op | source)
XLA Modules:
  0.0 390.6 jit_solution(13101071751127374768)
XLA Ops:
  10.3 5.1 %collective-permute-start = (bf16[4,96,768]{2,1,0:T(8,128)(2,1)S(1)}, bf16[4,96,768]{2,1,0:T(8,128)(2,1)S(1)}, u32[]{:S(2)}, u32[]{:S(2)}) collective-permute-start(bf16[4,96,768]{2,1,0:T(8,128)(2,1)S(1)} %get-tuple-element.175.refs_0_), channel_id=1, source_target_pairs={{0,1},{3,2},{4,5},{7,6},{8,9},{11,10},{12,13},{15,14},{16,17},{19,... | collective-permute-start | bytes 1769480 | tf_op jit(solution)/shard_map/ppermute | solution.py:854
  18.2 9.8 %collective-permute-done.refs_1_ = bf16[4,96,768]{2,1,0:T(8,128)(2,1)S(1)} collective-permute-done((bf16[4,96,768]{2,1,0:T(8,128)(2,1)S(1)}, bf16[4,96,768]{2,1,0:T(8,128)(2,1)S(1)}, u32[]{:S(2)}, u32[]{:S(2)}) %collective-permute-start) | collective-permute-done | bytes 589856 | tf_op jit(solution)/shard_map/ppermute | solution.py:854
  29.8 7.2 %collective-permute-start.3 = (bf16[4,96,768]{2,1,0:T(8,128)(2,1)S(1)}, bf16[4,96,768]{2,1,0:T(8,128)(2,1)S(1)}, u32[]{:S(2)}, u32[]{:S(2)}) collective-permute-start(bf16[4,96,768]{2,1,0:T(8,128)(2,1)S(1)} %get-tuple-element.181.refs_0_), channel_id=1, source_target_pairs={{0,1},{3,2},{4,5},{7,6},{8,9},{11,10},{12,13},{15,14},{16,17},{19,... | collective-permute-start | bytes 1769480 | tf_op jit(solution)/shard_map/ppermute | solution.py:854
  38.4 9.9 %collective-permute-done.3.refs_1_ = bf16[4,96,768]{2,1,0:T(8,128)(2,1)S(1)} collective-permute-done((bf16[4,96,768]{2,1,0:T(8,128)(2,1)S(1)}, bf16[4,96,768]{2,1,0:T(8,128)(2,1)S(1)}, u32[]{:S(2)}, u32[]{:S(2)}) %collective-permute-start.3) | collective-permute-done | bytes 589856 | tf_op jit(solution)/shard_map/ppermute | solution.py:854
  48.5 11.1 %collective-permute-done.2.refs_2_ = bf16[4,96,768]{2,1,0:T(8,128)(2,1)S(1)} collective-permute-done((bf16[4,96,768]{2,1,0:T(8,128)(2,1)S(1)}, bf16[4,96,768]{2,1,0:T(8,128)(2,1)S(1)}, u32[]{:S(2)}, u32[]{:S(2)}) %collective-permute-start.2) | collective-permute-done | bytes 589856 | tf_op jit(solution)/shard_map/ppermute | solution.py:854
  68.0 8.4 %collective-permute-done.4.refs_1_ = bf16[4,96,768]{2,1,0:T(8,128)(2,1)S(1)} collective-permute-done((bf16[4,96,768]{2,1,0:T(8,128)(2,1)S(1)}, bf16[4,96,768]{2,1,0:T(8,128)(2,1)S(1)}, u32[]{:S(2)}, u32[]{:S(2)}) %collective-permute-start.4) | collective-permute-done | bytes 589856 | tf_op jit(solution)/shard_map/ppermute | solution.py:854
  76.5 9.6 %collective-permute-done.7.refs_2_ = bf16[4,96,768]{2,1,0:T(8,128)(2,1)S(1)} collective-permute-done((bf16[4,96,768]{2,1,0:T(8,128)(2,1)S(1)}, bf16[4,96,768]{2,1,0:T(8,128)(2,1)S(1)}, u32[]{:S(2)}, u32[]{:S(2)}) %collective-permute-start.7) | collective-permute-done | bytes 589856 | tf_op jit(solution)/shard_map/ppermute | solution.py:854
  91.6 8.1 %all-gather.7.cloned.1.call-done = bf16[32,96,768]{2,1,0:T(8,128)(2,1)} async-done(((bf16[4,96,768]{2,1,0:T(8,128)(2,1)}), bf16[32,96,768]{2,1,0:T(8,128)(2,1)}) %all-gather.7.cloned.1.call-update) | async-done | bytes 4718608 | tf_op jit(solution)/shard_map/all_gather | solution.py:869
  99.7 12.3 %shard_map.232 = (bf16[1024,768]{1,0:T(8,128)(2,1)}, bf16[1024,768]{1,0:T(8,128)(2,1)}, f32[1,768]{1,0:T(1,128)}, bf16[4,2,96,768]{3,2,1,0:T(8,128)(2,1)}, bf16[...) custom-call(s32[1]{0:T(128)} %bitcast.refs_0_, bf16[1024,768]{1,0:T(8,128)(2,1)} %copy-done.49, bf16[1024,768]{1,0:T(8,128)(2,1)} %refs_7_.3, ...), custom_call_target="tpu_custom_call" | custom-call | flops 4831838208 | bytes 12582912 | tf_op jit(solution)/shard_map/pallas_call | solution.py:83
  112.0 12.5 %shard_map.233 = (bf16[1024,768]{1,0:T(8,128)(2,1)}, bf16[1024,768]{1,0:T(8,128)(2,1)}, f32[1,768]{1,0:T(1,128)}, bf16[4,2,96,768]{3,2,1,0:T(8,128)(2,1)}, bf16[...) custom-call(s32[1]{0:T(128)} %bitcast.refs_0_, bf16[1024,768]{1,0:T(8,128)(2,1)} %copy-done.49, bf16[1024,768]{1,0:T(8,128)(2,1)} %refs_7_.3, ...), custom_call_target="tpu_custom_call" | custom-call | flops 4831838208 | bytes 12582912 | tf_op jit(solution)/shard_map/pallas_call | solution.py:83
  142.9 12.3 %shard_map.236 = (bf16[1024,768]{1,0:T(8,128)(2,1)}, bf16[1024,768]{1,0:T(8,128)(2,1)}, bf16[1024,768]{1,0:T(8,128)(2,1)}, bf16[1024,768]{1,0:T(8,128)(2,1)}, f32[8,128]{1,0:T(8,128)}) custom-call(s32[1]{0:T(128)} %bitcast.refs_0_, bf16[1024,768]{1,0:T(8,128)(2,1)} %copy-done.50, bf16[1024,768]{1,0:T(8,128)(2,1)} %refs_7_.3, f32[3,768]{1,0:T(4,128)} %slice.18.refs_3_, ...), custom_call_target="tpu_custom_call" | custom-call | flops 4831838208 | bytes 15728640 | tf_op jit(solution)/shard_map/pallas_call | solution.py:83
  155.2 14.6 %shard_map.237 = (bf16[1024,768]{1,0:T(8,128)(2,1)}, bf16[1024,768]{1,0:T(8,128)(2,1)}, bf16[1024,768]{1,0:T(8,128)(2,1)}, bf16[1024,768]{1,0:T(8,128)(2,1)}, f32[1,3,768]{2,1,0:T(4,128)}, /*index=5*/f32[8,128]{1,0:T(8,128)}) custom-call(bf16[1024,768]{1,0:T(8,128)(2,1)} %get-tuple-element.207.refs_0_, bf16[1024,768]{1,0:T(8,128)(2,1)} %get-tuple-element.208.refs_1_, ...), custom_call_target="tpu_custom_call" | custom-call | flops 10000000000 | bytes 15728640 | tf_op jit(solution)/shard_map/pallas_call | solution.py:83
  169.8 14.7 %shard_map.238 = (bf16[1024,768]{1,0:T(8,128)(2,1)}, bf16[1024,768]{1,0:T(8,128)(2,1)}, bf16[1024,768]{1,0:T(8,128)(2,1)}, bf16[1024,768]{1,0:T(8,128)(2,1)}, f32[1,3,768]{2,1,0:T(4,128)}, /*index=5*/f32[8,128]{1,0:T(8,128)}) custom-call(bf16[1024,768]{1,0:T(8,128)(2,1)} %get-tuple-element.207, ...), custom_call_target="tpu_custom_call", output_to_operand_aliasing={{0}: (7, {}), {1}: (8, {}), {2}: (9, {}), {3}: (10, {})} | custom-call | flops 10000000000 | bytes 15728640 | tf_op jit(solution)/shard_map/pallas_call | solution.py:83
  188.0 11.2 %shard_map.240 = (bf16[4,4,96,768]{3,2,1,0:T(8,128)(2,1)}, bf16[4,4,96,768]{3,2,1,0:T(8,128)(2,1)}, f32[8,128]{1,0:T(8,128)}) custom-call(s32[1]{0:T(128)} %bitcast.refs_0_, bf16[1024,768]{1,0:T(8,128)(2,1)} %copy-done.50, bf16[1024,768]{1,0:T(8,128)(2,1)} %get-tuple-element.217.refs_2_.refs_1_, bf16[1024,768]{1,0:T(8,128)(2,1)} %refs_7_.3, ...), custom_call_target="tpu_custom_call" | custom-call | flops 4831838208 | bytes 9437184 | tf_op jit(solution)/shard_map/pallas_call | solution.py:83
  199.3 6.9 %collective-permute-start.15 = (bf16[4,96,768]{2,1,0:T(8,128)(2,1)S(1)}, bf16[4,96,768]{2,1,0:T(8,128)(2,1)}, u32[]{:S(2)}, u32[]{:S(2)}) collective-permute-start(bf16[4,96,768]{2,1,0:T(8,128)(2,1)S(1)} %get-tuple-element.229.refs_0_), channel_id=1, source_target_pairs={{0,1},{3,2},{4,5},{7,6},{8,9},{11,10},{12,13},{15,14},{16,17},{19,... | collective-permute-start | bytes 1769480 | tf_op jit(solution)/shard_map/ppermute | solution.py:854
  206.3 12.3 %shard_map.241 = (bf16[1024,768]{1,0:T(8,128)(2,1)}, bf16[1024,768]{1,0:T(8,128)(2,1)}, f32[1,768]{1,0:T(1,128)}, bf16[4,2,96,768]{3,2,1,0:T(8,128)(2,1)}, bf16[...) custom-call(s32[1]{0:T(128)} %bitcast.refs_0_, bf16[1024,768]{1,0:T(8,128)(2,1)} %copy-done.49, bf16[1024,768]{1,0:T(8,128)(2,1)} %refs_7_.3, ...), custom_call_target="tpu_custom_call" | custom-call | flops 4831838208 | bytes 12582912 | tf_op jit(solution)/shard_map/pallas_call | solution.py:83
  231.9 15.4 %shard_map.244 = (f32[1024,768]{1,0:T(8,128)}, f32[1024,768]{1,0:T(8,128)}, f32[5,768]{1,0:T(8,128)}, f32[8,128]{1,0:T(8,128)}) custom-call(s32[1]{0:T(128)} %bitcast.refs_0_, bf16[1024,768]{1,0:T(8,128)(2,1)} %get-tuple-element.217.refs_2_.refs_1_, bf16[1024,768]{1,0:T(8,128)(2,1)} %get-tuple-element.240.refs_2_, ...), custom_call_target="tpu_custom_call" | custom-call | flops 7247757312 | bytes 15728640 | tf_op jit(solution)/shard_map/pallas_call | solution.py:83
  252.2 5.9 %collective-permute-done.17.refs_2_ = bf16[4,96,768]{2,1,0:T(8,128)(2,1)} collective-permute-done((bf16[4,96,768]{2,1,0:T(8,128)(2,1)}, bf16[4,96,768]{2,1,0:T(8,128)(2,1)}, u32[]{:S(2)}, u32[]{:S(2)}) %collective-permute-start.17) | collective-permute-done | bytes 589856 | tf_op jit(solution)/shard_map/ppermute | solution.py:842
  260.4 5.9 %collective-permute-start.24 = (bf16[4,96,768]{2,1,0:T(8,128)(2,1)S(1)}, bf16[4,96,768]{2,1,0:T(8,128)(2,1)S(1)}, u32[]{:S(2)}, u32[]{:S(2)}) collective-permute-start(bf16[4,96,768]{2,1,0:T(8,128)(2,1)S(1)} %get-tuple-element.260.refs_0_), channel_id=1, source_target_pairs={{0,1},{3,2},{4,5},{7,6},{8,9},{11,10},{12,13},{15,14},{16,17},{19,... | collective-permute-start | bytes 1769480 | tf_op jit(solution)/shard_map/ppermute | solution.py:854
  269.9 12.3 %shard_map.248 = (bf16[1024,768]{1,0:T(8,128)(2,1)}, bf16[1024,768]{1,0:T(8,128)(2,1)}, f32[1,768]{1,0:T(1,128)}, bf16[4,2,96,768]{3,2,1,0:T(8,128)(2,1)}, bf16[...) custom-call(s32[1]{0:T(128)} %bitcast.refs_0_, bf16[1024,768]{1,0:T(8,128)(2,1)} %copy-done.49, bf16[1024,768]{1,0:T(8,128)(2,1)} %refs_7_.3, ...), custom_call_target="tpu_custom_call" | custom-call | flops 4831838208 | bytes 12582912 | tf_op jit(solution)/shard_map/pallas_call | solution.py:83
  296.0 10.7 %shard_map.253 = (f32[1024,768]{1,0:T(8,128)}, f32[1024,768]{1,0:T(8,128)}, f32[8,128]{1,0:T(8,128)}) custom-call(s32[1]{0:T(128)} %bitcast.refs_0_, bf16[1024,768]{1,0:T(8,128)(2,1)} %get-tuple-element.250.refs_1_, bf16[1024,768]{1,0:T(8,128)(2,1)} %get-tuple-element.251.refs_2_, bf16[1024,768]{1,0:T(8,128)(2,1)} %get-tuple-element.252.refs_3_, ...), custom_call_target="tpu_custom_call" | custom-call | flops 4831838208 | bytes 12582912 | tf_op jit(solution)/shard_map/pallas_call | solution.py:83
  322.1 12.7 %shard_map.257 = (bf16[1024,768]{1,0:T(8,128)(2,1)}, f32[1024,768]{1,0:T(8,128)}, f32[2,768]{1,0:T(2,128)}, f32[8,128]{1,0:T(8,128)}) custom-call(s32[1]{0:T(128)} %bitcast.refs_0_, bf16[1024,768]{1,0:T(8,128)(2,1)} %get-tuple-element.247.refs_1_, bf16[1024,768]{1,0:T(8,128)(2,1)} %get-tuple-element.248.refs_2_, f32[1024,768]{1,0:T(8,128)} %get-tuple-element.249.refs_3_, ...), custom_call_target="tpu_custom_call" | custom-call | flops 2415919104 | bytes 9437184 | tf_op jit(solution)/shard_map/pallas_call | solution.py:83
  352.6 6.6 %collective-permute-start.41 = (f32[13,768]{1,0:T(8,128)S(1)}, f32[13,768]{1,0:T(8,128)S(1)}, u32[]{:S(2)}, u32[]{:S(2)}) collective-permute-start(f32[13,768]{1,0:T(8,128)S(1)} %get-tuple-element.313.refs_0_), channel_id=1, source_target_pairs={{0,1},{1,0},{2,3},{3,2},{4,5},{5,4},{6,7},{7,6},{8,9},{9,8},{10,11... | collective-permute-start | bytes 119816 | tf_op jit(solution)/shard_map/ppermute | solution.py:842
  378.2 5.6 %shard_map.271 = (f32[1,1]{1,0:T(1,128)}, f32[13,768]{1,0:T(8,128)}, f32[13,768]{1,0:T(8,128)}, f32[13,768]{1,0:T(8,128)}, f32[13,768]{1,0:T(8,128)}, /*index=5*...) custom-call(s32[3,6]{1,0:T(4,128)S(1)} %pad_add_fusion.src_ref, ...), custom_call_target="tpu_custom_call" | custom-call | flops 8847360 | bytes 14155776 | tf_op jit(solution)/shard_map/pallas_call | solution.py:663
  (266 shorter events, 133.8 us)
Async XLA Ops:
  7.2 92.6 %all-gather.7.cloned.1.call-start = ((), (), s32[]{:S(2)}) async-start(), calls=%async_computation | async-start | bytes 5308416 | tf_op jit(solution)/shard_map/all_gather | solution.py:869
  29.8 18.6 %collective-permute-start.3 = (bf16[4,96,768]{2,1,0:T(8,128)(2,1)S(1)}, bf16[4,96,768]{2,1,0:T(8,128)(2,1)S(1)}, u32[]{:S(2)}, u32[]{:S(2)}) collective-permute-start(bf16[4,96,768]{2,1,0:T(8,128)(2,1)S(1)} %get-tuple-element.181.refs_0_), channel_id=1, source_target_pairs={{0,1},{3,2},{4,5},{7,6},{8,9},{11,10},{12,13},{15,14},{16,17},{19,... | collective-permute-start | bytes 1769480 | tf_op jit(solution)/shard_map/ppermute | solution.py:854
  37.1 22.5 %collective-permute-start.2 = (bf16[4,96,768]{2,1,0:T(8,128)(2,1)S(1)}, bf16[4,96,768]{2,1,0:T(8,128)(2,1)S(1)}, u32[]{:S(2)}, u32[]{:S(2)}) collective-permute-start(bf16[4,96,768]{2,1,0:T(8,128)(2,1)S(1)} %get-tuple-element.180.refs_1_), channel_id=1, source_target_pairs={{1,0},{2,3},{5,4},{6,7},{9,8},{10,11},{13,12},{14,15},{17,16},{18,... | collective-permute-start | bytes 1769480 | tf_op jit(solution)/shard_map/ppermute | solution.py:854
  60.5 82.4 %all-gather.11.cloned.1.call-start = ((), (), s32[]{:S(2)}) async-start(), calls=%async_computation.2 | async-start | bytes 5308416 | tf_op jit(solution)/shard_map/all_gather | solution.py:869
  66.7 19.4 %collective-permute-start.7 = (bf16[4,96,768]{2,1,0:T(8,128)(2,1)S(1)}, bf16[4,96,768]{2,1,0:T(8,128)(2,1)S(1)}, u32[]{:S(2)}, u32[]{:S(2)}) collective-permute-start(bf16[4,96,768]{2,1,0:T(8,128)(2,1)S(1)} %get-tuple-element.190.refs_1_), channel_id=1, source_target_pairs={{1,0},{2,3},{5,4},{6,7},{9,8},{10,11},{13,12},{14,15},{17,16},{18,... | collective-permute-start | bytes 1769480 | tf_op jit(solution)/shard_map/ppermute | solution.py:854
  87.0 119.3 %all-gather.9.cloned.1.call-start = ((), (), s32[]{:S(2)}) async-start(), calls=%async_computation.1 | async-start | bytes 5308416 | tf_op jit(solution)/shard_map/all_gather | solution.py:869
  89.9 34.7 %collective-permute-start.8 = (bf16[4,96,768]{2,1,0:T(8,128)(2,1)}, bf16[4,96,768]{2,1,0:T(8,128)(2,1)}, u32[]{:S(2)}, u32[]{:S(2)}) collective-permute-start(bf16[4,96,768]{2,1,0:T(8,128)(2,1)} %get-tuple-element.193.refs_1_), channel_id=1, source_target_pairs={{1,0},{2,3},{5,4},{6,7},{9,8},{10,11},{13,12},{14,15},{17,16},{18,... | collective-permute-start | bytes 1769480 | tf_op jit(solution)/shard_map/ppermute | solution.py:854
  139.4 45.1 %collective-permute-start.11 = (bf16[4,96,768]{2,1,0:T(8,128)(2,1)}, bf16[4,96,768]{2,1,0:T(8,128)(2,1)S(1)}, u32[]{:S(2)}, u32[]{:S(2)}) collective-permute-start(bf16[4,96,768]{2,1,0:T(8,128)(2,1)} %get-tuple-element.222), channel_id=1, source_target_pairs={{0,8},{4,12},{8,0},{12,4},{16,24},{20,28},{24,16},{28,20},{1,9},{5... | collective-permute-start | bytes 1769480 | tf_op jit(solution)/shard_map/ppermute | solution.py:842
  140.9 43.6 %collective-permute-start.12 = (bf16[4,96,768]{2,1,0:T(8,128)(2,1)}, bf16[4,96,768]{2,1,0:T(8,128)(2,1)S(1)}, u32[]{:S(2)}, u32[]{:S(2)}) collective-permute-start(bf16[4,96,768]{2,1,0:T(8,128)(2,1)} %get-tuple-element.223), channel_id=1, source_target_pairs={{0,16},{4,20},{8,24},{12,28},{16,0},{20,4},{24,8},{28,12},{1,17},{... | collective-permute-start | bytes 1769480 | tf_op jit(solution)/shard_map/ppermute | solution.py:842
  141.8 42.7 %collective-permute-start.13 = (bf16[4,96,768]{2,1,0:T(8,128)(2,1)}, bf16[4,96,768]{2,1,0:T(8,128)(2,1)S(1)}, u32[]{:S(2)}, u32[]{:S(2)}) collective-permute-start(bf16[4,96,768]{2,1,0:T(8,128)(2,1)} %get-tuple-element.224), channel_id=1, source_target_pairs={{0,24},{4,28},{8,16},{12,20},{16,8},{20,12},{24,0},{28,4},{1,25},{... | collective-permute-start | bytes 1769480 | tf_op jit(solution)/shard_map/ppermute | solution.py:842
  199.2 22.3 %collective-permute-start.14 = (bf16[4,4,96,768]{3,2,1,0:T(8,128)(2,1)}, bf16[4,4,96,768]{3,2,1,0:T(8,128)(2,1)}, u32[]{:S(2)}, u32[]{:S(2)}) collective-permute-start(bf16[4,4,96,768]{3,2,1,0:T(8,128)(2,1)} %get-tuple-element.228), channel_id=1, source_target_pairs={{0,4},{4,0},{8,12},{12,8},{16,20},{20,16},{24,28},{28,24},{1,5},{5... | collective-permute-start | bytes 7077896 | tf_op jit(solution)/shard_map/ppermute | solution.py:842
  199.3 19.6 %collective-permute-start.15 = (bf16[4,96,768]{2,1,0:T(8,128)(2,1)S(1)}, bf16[4,96,768]{2,1,0:T(8,128)(2,1)}, u32[]{:S(2)}, u32[]{:S(2)}) collective-permute-start(bf16[4,96,768]{2,1,0:T(8,128)(2,1)S(1)} %get-tuple-element.229.refs_0_), channel_id=1, source_target_pairs={{0,1},{3,2},{4,5},{7,6},{8,9},{11,10},{12,13},{15,14},{16,17},{19,... | collective-permute-start | bytes 1769480 | tf_op jit(solution)/shard_map/ppermute | solution.py:854
  218.6 31.5 %collective-permute-start.19 = (bf16[4,2,96,768]{3,2,1,0:T(8,128)(2,1)}, bf16[4,2,96,768]{3,2,1,0:T(8,128)(2,1)S(1)}, u32[]{:S(2)}, u32[]{:S(2)}) collective-permute-start(bf16[4,2,96,768]{3,2,1,0:T(8,128)(2,1)} %get-tuple-element.238), channel_id=1, source_target_pairs={{0,4},{4,0},{8,12},{12,8},{16,20},{20,16},{24,28},{28,24},{1,5},{5... | collective-permute-start | bytes 3538952 | tf_op jit(solution)/shard_map/ppermute | solution.py:842
  220.7 26.6 %collective-permute-start.20 = (bf16[4,96,768]{2,1,0:T(8,128)(2,1)S(1)}, bf16[4,96,768]{2,1,0:T(8,128)(2,1)S(1)}, u32[]{:S(2)}, u32[]{:S(2)}) collective-permute-start(bf16[4,96,768]{2,1,0:T(8,128)(2,1)S(1)} %get-tuple-element.239.refs_0_), channel_id=1, source_target_pairs={{1,2},{2,1},{5,6},{6,5},{9,10},{10,9},{13,14},{14,13},{17,18},{18,... | collective-permute-start | bytes 1769480 | tf_op jit(solution)/shard_map/ppermute | solution.py:854
  228.4 23.8 %collective-permute-start.16 = (bf16[4,96,768]{2,1,0:T(8,128)(2,1)}, bf16[4,96,768]{2,1,0:T(8,128)(2,1)}, u32[]{:S(2)}, u32[]{:S(2)}) collective-permute-start(bf16[4,96,768]{2,1,0:T(8,128)(2,1)} %get-tuple-element.234), channel_id=1, source_target_pairs={{0,8},{4,12},{8,0},{12,4},{16,24},{20,28},{24,16},{28,20},{1,9},{5... | collective-permute-start | bytes 1769480 | tf_op jit(solution)/shard_map/ppermute | solution.py:842
  229.9 28.2 %collective-permute-start.17 = (bf16[4,96,768]{2,1,0:T(8,128)(2,1)}, bf16[4,96,768]{2,1,0:T(8,128)(2,1)}, u32[]{:S(2)}, u32[]{:S(2)}) collective-permute-start(bf16[4,96,768]{2,1,0:T(8,128)(2,1)} %get-tuple-element.235), channel_id=1, source_target_pairs={{0,16},{4,20},{8,24},{12,28},{16,0},{20,4},{24,8},{28,12},{1,17},{... | collective-permute-start | bytes 1769480 | tf_op jit(solution)/shard_map/ppermute | solution.py:842
  231.6 26.6 %collective-permute-start.18 = (bf16[4,96,768]{2,1,0:T(8,128)(2,1)}, bf16[4,96,768]{2,1,0:T(8,128)(2,1)}, u32[]{:S(2)}, u32[]{:S(2)}) collective-permute-start(bf16[4,96,768]{2,1,0:T(8,128)(2,1)} %get-tuple-element.236), channel_id=1, source_target_pairs={{0,24},{4,28},{8,16},{12,20},{16,8},{20,12},{24,0},{28,4},{1,25},{... | collective-permute-start | bytes 1769480 | tf_op jit(solution)/shard_map/ppermute | solution.py:842
  260.4 21.8 %collective-permute-start.24 = (bf16[4,96,768]{2,1,0:T(8,128)(2,1)S(1)}, bf16[4,96,768]{2,1,0:T(8,128)(2,1)S(1)}, u32[]{:S(2)}, u32[]{:S(2)}) collective-permute-start(bf16[4,96,768]{2,1,0:T(8,128)(2,1)S(1)} %get-tuple-element.260.refs_0_), channel_id=1, source_target_pairs={{0,1},{3,2},{4,5},{7,6},{8,9},{11,10},{12,13},{15,14},{16,17},{19,... | collective-permute-start | bytes 1769480 | tf_op jit(solution)/shard_map/ppermute | solution.py:854
  286.2 28.7 %collective-permute-start.27 = (bf16[4,96,768]{2,1,0:T(8,128)(2,1)S(1)}, bf16[4,96,768]{2,1,0:T(8,128)(2,1)S(1)}, u32[]{:S(2)}, u32[]{:S(2)}) collective-permute-start(bf16[4,96,768]{2,1,0:T(8,128)(2,1)S(1)} %get-tuple-element.271.refs_0_), channel_id=1, source_target_pairs={{1,2},{2,1},{5,6},{6,5},{9,10},{10,9},{13,14},{14,13},{17,18},{18,... | collective-permute-start | bytes 1769480 | tf_op jit(solution)/shard_map/ppermute | solution.py:854
  286.9 30.1 %collective-permute-start.26 = (bf16[2,96,768]{2,1,0:T(8,128)(2,1)}, bf16[2,96,768]{2,1,0:T(8,128)(2,1)}, u32[]{:S(2)}, u32[]{:S(2)}) collective-permute-start(bf16[2,96,768]{2,1,0:T(8,128)(2,1)} %get-tuple-element.270.refs_0_), channel_id=1, source_target_pairs={{0,1},{3,2},{4,5},{7,6},{8,9},{11,10},{12,13},{15,14},{16,17},{19,... | collective-permute-start | bytes 884744 | tf_op jit(solution)/shard_map/ppermute | solution.py:854
  311.7 29.4 %collective-permute-start.34 = (bf16[2,96,768]{2,1,0:T(8,128)(2,1)}, bf16[2,96,768]{2,1,0:T(8,128)(2,1)}, u32[]{:S(2)}, u32[]{:S(2)}) collective-permute-start(bf16[2,96,768]{2,1,0:T(8,128)(2,1)} %get-tuple-element.294.refs_0_), channel_id=1, source_target_pairs={{0,1},{3,2},{4,5},{7,6},{8,9},{11,10},{12,13},{15,14},{16,17},{19,... | collective-permute-start | bytes 884744 | tf_op jit(solution)/shard_map/ppermute | solution.py:854
  313.7 46.7 %collective-permute-start.31 = (bf16[4,96,768]{2,1,0:T(8,128)(2,1)S(1)}, bf16[4,96,768]{2,1,0:T(8,128)(2,1)S(1)}, u32[]{:S(2)}, u32[]{:S(2)}) collective-permute-start(bf16[4,96,768]{2,1,0:T(8,128)(2,1)S(1)} %get-tuple-element.282.refs_1_), channel_id=1, source_target_pairs={{1,0},{2,3},{5,4},{6,7},{9,8},{10,11},{13,12},{14,15},{17,16},{18,... | collective-permute-start | bytes 1769480 | tf_op jit(solution)/shard_map/ppermute | solution.py:854
  319.4 23.6 %collective-permute-start.33 = (bf16[2,96,768]{2,1,0:T(8,128)(2,1)}, bf16[2,96,768]{2,1,0:T(8,128)(2,1)}, u32[]{:S(2)}, u32[]{:S(2)}) collective-permute-start(bf16[2,96,768]{2,1,0:T(8,128)(2,1)} %get-tuple-element.293.refs_0_), channel_id=1, source_target_pairs={{1,2},{2,1},{5,6},{6,5},{9,10},{10,9},{13,14},{14,13},{17,18},{18,... | collective-permute-start | bytes 884744 | tf_op jit(solution)/shard_map/ppermute | solution.py:854
  320.8 40.0 %collective-permute-start.38 = (bf16[4,96,768]{2,1,0:T(8,128)(2,1)S(1)}, bf16[4,96,768]{2,1,0:T(8,128)(2,1)S(1)}, u32[]{:S(2)}, u32[]{:S(2)}) collective-permute-start(bf16[4,96,768]{2,1,0:T(8,128)(2,1)S(1)} %get-tuple-element.306.refs_1_), channel_id=1, source_target_pairs={{1,0},{2,3},{5,4},{6,7},{9,8},{10,11},{13,12},{14,15},{17,16},{18,... | collective-permute-start | bytes 1769480 | tf_op jit(solution)/shard_map/ppermute | solution.py:854
  (85 other events, 531.7 us)
Sparse Core Ops, SparseCore 0:
  60.7 39.0 all-gather.6
  101.6 38.9 all-gather.10
  143.0 55.8 all-gather.8
where the time goes:
time: 396 us; the launch traced here: 391 us
  Pallas kernels  179 us (45%)
  waiting for transfers between devices  82.7 us (21%)
  starting transfers between devices  78.8 us (20%)
  local copies, waits for them, and re-layouts  32.7 us (8%)
  between operations  15.6 us (4%)
    pallas_call x51, Pallas kernels, run(): *out, token = call(*args, *deps)  174 us
    ppermute x21, waiting for transfers between devices, hop(): return lax.ppermute(value, 'narrow', pairs)  50.6 us
    ppermute x21, starting transfers between devices, hop(): return lax.ppermute(value, 'narrow', pairs)  50.1 us
    unnamed x120, local copies, waits for them, and re-layouts  30.9 us
    ppermute x25, starting transfers between devices, swap(): return lax.ppermute(value, axis, [(i, i ^ bit) for i in range(size)])  28.5 us
    ppermute x25, waiting for transfers between devices, swap(): return lax.ppermute(value, axis, [(i, i ^ bit) for i in range(size)])  23.9 us
    all_gather x3, waiting for transfers between devices, gather_wide(): full = lax.all_gather(value, 'wide', axis=0, tiled=False)  8.12 us
  transfers between devices with their start and end apart: 49, of which 19 were waited for; matrix products, arithmetic and copies ran while one was open for 1% of the time, Pallas kernels for 43%

commit v1 on v0

--- a/solution.py
+++ b/solution.py
@@ -811,16 +811,15 @@
     )(here, value, outer)
 
 
-def settled(here, value, outer):
+def settled(value, other):
     count, rows, _ = value.shape
 
-    def body(h_ref, v_ref, o_ref, out_ref, q_ref):
-        ends = (h_ref[0] == 0) | (h_ref[0] == 3)
+    def body(v_ref, o_ref, out_ref, q_ref):
         total = jnp.zeros((8, 128), F32)
         for n in range(count):
-            kept = jnp.where(ends, o_ref[n], v_ref[n])
-            out_ref[n] = kept
-            x = kept.astype(F32)
+            low = (v_ref[n].astype(F32) + o_ref[n].astype(F32)).astype(BF)
+            out_ref[n] = low
+            x = low.astype(F32)
             x = x * x
             for c in range(D // 128):
                 part = x[:, c * 128 : (c + 1) * 128]
@@ -830,11 +829,11 @@
 
     return ordered(
         body,
-        in_specs=[SMEM, VMEM, VMEM],
+        in_specs=[VMEM, VMEM],
         out_specs=[VMEM, VMEM],
         out_shape=[jax.ShapeDtypeStruct(value.shape, BF), jax.ShapeDtypeStruct((8, 128), F32)],
         **params(16, 1, 1),
-    )(here, value, outer)
+    )(value, other)
 
 
 def swap(value, axis, bit):
@@ -855,6 +854,16 @@
     if pairs is INWARD:
         return (lax.psum(value.astype(F32), "narrow") - value.astype(F32)).astype(BF)
     return jnp.zeros_like(value) if pairs is ACROSS else value
+
+
+def near(value):
+    if lax.axis_size("narrow") == 4:
+        return swap(value, "narrow", 1)
+    return (lax.psum(value.astype(F32), "narrow") - value.astype(F32)).astype(BF)
+
+
+def far(value):
+    return swap(value, "narrow", 2) if lax.axis_size("narrow") == 4 else jnp.zeros_like(value)
 
 
 def spread_wide(value):
@@ -1005,11 +1014,11 @@
         q, k, v, da, start, cosine, sine, length, tuple(range(half, seqs)), into=inner
     )
     front = total_of(front)
-    r_f = hop(front, INWARD)
+    r_f = near(front)
     s_s = give(attention_grads(me, h_one, a, cotangent, dqkv, four_outs, four_plan))
     s_2 = give(chunk(2))
     front = total_of([front, r_f])
-    r_f = hop(front, ACROSS)
+    r_f = far(front)
     mid = exchange(s_s)
     middle, e_part, sums = products(
         me,
@@ -1022,24 +1031,21 @@
         [full, full, jax.ShapeDtypeStruct((5, D), F32)],
         extra=[(tokens, True), (cotangent, True), (vectors, False)],
     )
-    front = total_of([front, r_f])
-    r_f = hop(front, OUTWARD)
     third = exchange(s_2)
     mid = total_of(mid)
-    r_m = hop(mid, INWARD)
+    r_m = near(mid)
     s_3 = chunk(3)
     mid = total_of([mid, r_m])
-    r_m = hop(mid, ACROSS)
+    r_m = far(mid)
+    front, front_square = settled(front, r_f)
     third = total_of(third)
-    r_h = hop(third, INWARD)
+    r_h = near(third)
     last = exchange(give([*s_3[:-1], handed_on(s_3[-1])]))
     early = products(me, [[forth(0), forth(1)], [back(0), back(1)]], store_all, [full, full])
     last = total_of(last)
-    r_l = hop(last, INWARD)
-    mid = total_of([mid, r_m])
-    r_m = hop(mid, OUTWARD)
+    r_l = near(last)
     third = total_of([third, r_h])
-    r_h = hop(third, ACROSS)
+    r_h = far(third)
     layer_out, input_grad, last_sums = products(
         me,
         [[forth(3)], [back(3)]],
@@ -1048,27 +1054,21 @@
         starts=[(middle, early[0]), (early[1],)],
         extra=[(tokens, True), (cotangent, True), (vectors, False), (e_part, True)],
     )
+    last = total_of([last, r_l])
+    r_l = far(last)
+    third, third_square = settled(third, r_h)
+    mid, mid_square = settled(mid, r_m)
     vector_total = vector_terms(sums, last_sums, db_a, db_b, dbs)
     masks = [(axis, 1 << n) for axis in ("wide", "narrow") for n in range(lax.axis_size(axis).bit_length() - 1)]
 
     def vector_step(value):
         return plus(value, swap(value, *masks.pop(0)))
 
-    last = total_of([last, r_l])
-    r_l = hop(last, ACROSS)
-    third = total_of([third, r_h])
-    r_h = hop(third, OUTWARD)
-    vector_total = vector_step(vector_total)
-    vector_total = vector_step(vector_total)
-    last = total_of([last, r_l])
-    r_l = hop(last, OUTWARD)
-    vector_total = vector_step(vector_total)
-    front, front_square = settled(here, front, r_f)
-    mid, mid_square = settled(here, mid, r_m)
-    third, third_square = settled(here, third, r_h)
+    while masks[0][0] == "wide":
+        vector_total = vector_step(vector_total)
+    last, last_square = settled(last, r_l)
     while masks:
         vector_total = vector_step(vector_total)
-    last, last_square = settled(here, last, r_l)
     squares = total_axis(front_square + mid_square + third_square + last_square, "wide")
     summed = (front, mid, third, last)
     held = ((4, 8, 5, 9), ids_s, (6, 10), (7, 11))

time: 396 us -> 382 us (0.965)
  starting transfers between devices: 78.8 us -> 54.9 us
  waiting for transfers between devices: 82.7 us -> 95.6 us
    ppermute x21 -> x9, starting transfers between devices: 50.1 us -> 22.7 us  [hop(): return lax.ppermute(value, 'narrow', pairs)]
    ppermute x25 -> x33, waiting for transfers between devices: 23.9 us -> 38.6 us  [swap(): return lax.ppermute(value, axis, [(i, i ^ bit) for i in range(size)])]
    ppermute x25 -> x33, starting transfers between devices: 28.5 us -> 32 us  [swap(): return lax.ppermute(value, axis, [(i, i ^ bit) for i in range(size)])]
    unnamed x120 -> x118, local copies, waits for them, and re-layouts: 30.9 us -> 28.1 us
    ppermute x21 -> x9, waiting for transfers between devices: 50.6 us -> 48.8 us  [hop(): return lax.ppermute(value, 'narrow', pairs)]
    pallas_call x51 -> x47, Pallas kernels: 174 us -> 173 us  [run(): *out, token = call(*args, *deps)]
  transfers between devices with their start and end apart: 49 -> 45, of which waited for: 19 -> 22; matrix products, arithmetic and copies ran while one was open for 1% -> 1% of each run, Pallas kernels for 43% -> 44%
where the time goes in v1:
time: 382 us; the launch traced here: 377 us
  Pallas kernels  179 us (47%)
  waiting for transfers between devices  95.6 us (25%)
  starting transfers between devices  54.9 us (14%)
  local copies, waits for them, and re-layouts  29.9 us (8%)
  between operations  15.5 us (4%)
    pallas_call x47, Pallas kernels, run(): *out, token = call(*args, *deps)  173 us
    ppermute x9, waiting for transfers between devices, hop(): return lax.ppermute(value, 'narrow', pairs)  48.8 us
    ppermute x33, waiting for transfers between devices, swap(): return lax.ppermute(value, axis, [(i, i ^ bit) for i in range(size)])  38.6 us
    ppermute x33, starting transfers between devices, swap(): return lax.ppermute(value, axis, [(i, i ^ bit) for i in range(size)])  32 us
    unnamed x118, local copies, waits for them, and re-layouts  28.1 us
    ppermute x9, starting transfers between devices, hop(): return lax.ppermute(value, 'narrow', pairs)  22.7 us
    all_gather x3, waiting for transfers between devices, gather_wide(): full = lax.all_gather(value, 'wide', axis=0, tiled=False)  8.28 us
  transfers between devices with their start and end apart: 45, of which 22 were waited for; matrix products, arithmetic and copies ran while one was open for 1% of the time, Pallas kernels for 44%

profile of v1, /device:TPU:0, one launch (start us, length us, event | category | flops | bytes accessed | tf_op | source)
XLA Modules:
  0.0 377.1 jit_solution(5528230530194601543)
XLA Ops:
  10.3 5.1 %collective-permute-start = (bf16[4,96,768]{2,1,0:T(8,128)(2,1)S(1)}, bf16[4,96,768]{2,1,0:T(8,128)(2,1)S(1)}, u32[]{:S(2)}, u32[]{:S(2)}) collective-permute-start(bf16[4,96,768]{2,1,0:T(8,128)(2,1)S(1)} %get-tuple-element.167.refs_0_), channel_id=1, source_target_pairs={{0,1},{3,2},{4,5},{7,6},{8,9},{11,10},{12,13},{15,14},{16,17},{19,... | collective-permute-start | bytes 1769480 | tf_op jit(solution)/shard_map/ppermute | solution.py:853
  18.2 9.8 %collective-permute-done.refs_1_ = bf16[4,96,768]{2,1,0:T(8,128)(2,1)S(1)} collective-permute-done((bf16[4,96,768]{2,1,0:T(8,128)(2,1)S(1)}, bf16[4,96,768]{2,1,0:T(8,128)(2,1)S(1)}, u32[]{:S(2)}, u32[]{:S(2)}) %collective-permute-start) | collective-permute-done | bytes 589856 | tf_op jit(solution)/shard_map/ppermute | solution.py:853
  29.8 7.2 %collective-permute-start.3 = (bf16[4,96,768]{2,1,0:T(8,128)(2,1)S(1)}, bf16[4,96,768]{2,1,0:T(8,128)(2,1)S(1)}, u32[]{:S(2)}, u32[]{:S(2)}) collective-permute-start(bf16[4,96,768]{2,1,0:T(8,128)(2,1)S(1)} %get-tuple-element.173.refs_0_), channel_id=1, source_target_pairs={{0,1},{3,2},{4,5},{7,6},{8,9},{11,10},{12,13},{15,14},{16,17},{19,... | collective-permute-start | bytes 1769480 | tf_op jit(solution)/shard_map/ppermute | solution.py:853
  38.4 9.9 %collective-permute-done.3.refs_1_ = bf16[4,96,768]{2,1,0:T(8,128)(2,1)S(1)} collective-permute-done((bf16[4,96,768]{2,1,0:T(8,128)(2,1)S(1)}, bf16[4,96,768]{2,1,0:T(8,128)(2,1)S(1)}, u32[]{:S(2)}, u32[]{:S(2)}) %collective-permute-start.3) | collective-permute-done | bytes 589856 | tf_op jit(solution)/shard_map/ppermute | solution.py:853
  48.5 11.1 %collective-permute-done.2.refs_2_ = bf16[4,96,768]{2,1,0:T(8,128)(2,1)S(1)} collective-permute-done((bf16[4,96,768]{2,1,0:T(8,128)(2,1)S(1)}, bf16[4,96,768]{2,1,0:T(8,128)(2,1)S(1)}, u32[]{:S(2)}, u32[]{:S(2)}) %collective-permute-start.2) | collective-permute-done | bytes 589856 | tf_op jit(solution)/shard_map/ppermute | solution.py:853
  62.2 4.3 %collective-permute-start.4 = (bf16[4,96,768]{2,1,0:T(8,128)(2,1)S(1)}, bf16[4,96,768]{2,1,0:T(8,128)(2,1)S(1)}, u32[]{:S(2)}, u32[]{:S(2)}) collective-permute-start(bf16[4,96,768]{2,1,0:T(8,128)(2,1)S(1)} %get-tuple-element.177.refs_0_), channel_id=1, source_target_pairs={{0,1},{3,2},{4,5},{7,6},{8,9},{11,10},{12,13},{15,14},{16,17},{19,... | collective-permute-start | bytes 1769480 | tf_op jit(solution)/shard_map/ppermute | solution.py:853
  68.0 8.4 %collective-permute-done.4.refs_1_ = bf16[4,96,768]{2,1,0:T(8,128)(2,1)S(1)} collective-permute-done((bf16[4,96,768]{2,1,0:T(8,128)(2,1)S(1)}, bf16[4,96,768]{2,1,0:T(8,128)(2,1)S(1)}, u32[]{:S(2)}, u32[]{:S(2)}) %collective-permute-start.4) | collective-permute-done | bytes 589856 | tf_op jit(solution)/shard_map/ppermute | solution.py:853
  76.5 9.6 %collective-permute-done.7.refs_2_ = bf16[4,96,768]{2,1,0:T(8,128)(2,1)S(1)} collective-permute-done((bf16[4,96,768]{2,1,0:T(8,128)(2,1)S(1)}, bf16[4,96,768]{2,1,0:T(8,128)(2,1)S(1)}, u32[]{:S(2)}, u32[]{:S(2)}) %collective-permute-start.7) | collective-permute-done | bytes 589856 | tf_op jit(solution)/shard_map/ppermute | solution.py:853
  91.4 8.3 %all-gather.7.cloned.1.call-done = bf16[32,96,768]{2,1,0:T(8,128)(2,1)} async-done(((bf16[4,96,768]{2,1,0:T(8,128)(2,1)}), bf16[32,96,768]{2,1,0:T(8,128)(2,1)}) %all-gather.7.cloned.1.call-update) | async-done | bytes 4718608 | tf_op jit(solution)/shard_map/all_gather | solution.py:878
  99.7 12.3 %shard_map.232 = (bf16[1024,768]{1,0:T(8,128)(2,1)}, bf16[1024,768]{1,0:T(8,128)(2,1)}, f32[1,768]{1,0:T(1,128)}, bf16[4,2,96,768]{3,2,1,0:T(8,128)(2,1)}, bf16[...) custom-call(s32[1]{0:T(128)} %bitcast.refs_0_, bf16[1024,768]{1,0:T(8,128)(2,1)} %copy-done.48, bf16[1024,768]{1,0:T(8,128)(2,1)} %refs_7_.3, ...), custom_call_target="tpu_custom_call" | custom-call | flops 4831838208 | bytes 12582912 | tf_op jit(solution)/shard_map/pallas_call | solution.py:83
  112.0 12.6 %shard_map.233 = (bf16[1024,768]{1,0:T(8,128)(2,1)}, bf16[1024,768]{1,0:T(8,128)(2,1)}, f32[1,768]{1,0:T(1,128)}, bf16[4,2,96,768]{3,2,1,0:T(8,128)(2,1)}, bf16[...) custom-call(s32[1]{0:T(128)} %bitcast.refs_0_, bf16[1024,768]{1,0:T(8,128)(2,1)} %copy-done.48, bf16[1024,768]{1,0:T(8,128)(2,1)} %refs_7_.3, ...), custom_call_target="tpu_custom_call" | custom-call | flops 4831838208 | bytes 12582912 | tf_op jit(solution)/shard_map/pallas_call | solution.py:83
  143.0 12.3 %shard_map.236 = (bf16[1024,768]{1,0:T(8,128)(2,1)}, bf16[1024,768]{1,0:T(8,128)(2,1)}, bf16[1024,768]{1,0:T(8,128)(2,1)}, bf16[1024,768]{1,0:T(8,128)(2,1)}, f32[8,128]{1,0:T(8,128)}) custom-call(s32[1]{0:T(128)} %bitcast.refs_0_, bf16[1024,768]{1,0:T(8,128)(2,1)} %copy-done.49, bf16[1024,768]{1,0:T(8,128)(2,1)} %refs_7_.3, f32[3,768]{1,0:T(4,128)} %slice.18.refs_3_, ...), custom_call_target="tpu_custom_call" | custom-call | flops 4831838208 | bytes 15728640 | tf_op jit(solution)/shard_map/pallas_call | solution.py:83
  155.3 14.6 %shard_map.237 = (bf16[1024,768]{1,0:T(8,128)(2,1)}, bf16[1024,768]{1,0:T(8,128)(2,1)}, bf16[1024,768]{1,0:T(8,128)(2,1)}, bf16[1024,768]{1,0:T(8,128)(2,1)}, f32[1,3,768]{2,1,0:T(4,128)}, /*index=5*/f32[8,128]{1,0:T(8,128)}) custom-call(bf16[1024,768]{1,0:T(8,128)(2,1)} %get-tuple-element.199.refs_0_, bf16[1024,768]{1,0:T(8,128)(2,1)} %get-tuple-element.200.refs_1_, ...), custom_call_target="tpu_custom_call" | custom-call | flops 10000000000 | bytes 15728640 | tf_op jit(solution)/shard_map/pallas_call | solution.py:83
  170.0 15.1 %shard_map.238 = (bf16[1024,768]{1,0:T(8,128)(2,1)}, bf16[1024,768]{1,0:T(8,128)(2,1)}, bf16[1024,768]{1,0:T(8,128)(2,1)}, bf16[1024,768]{1,0:T(8,128)(2,1)}, f32[1,3,768]{2,1,0:T(4,128)}, /*index=5*/f32[8,128]{1,0:T(8,128)}) custom-call(bf16[1024,768]{1,0:T(8,128)(2,1)} %get-tuple-element.199, ...), custom_call_target="tpu_custom_call", output_to_operand_aliasing={{0}: (7, {}), {1}: (8, {}), {2}: (9, {}), {3}: (10, {})} | custom-call | flops 10000000000 | bytes 15728640 | tf_op jit(solution)/shard_map/pallas_call | solution.py:83
  189.6 11.0 %shard_map.240 = (bf16[4,4,96,768]{3,2,1,0:T(8,128)(2,1)}, bf16[4,4,96,768]{3,2,1,0:T(8,128)(2,1)}, f32[8,128]{1,0:T(8,128)}) custom-call(s32[1]{0:T(128)} %bitcast.refs_0_, bf16[1024,768]{1,0:T(8,128)(2,1)} %copy-done.49, bf16[1024,768]{1,0:T(8,128)(2,1)} %get-tuple-element.209.refs_2_.refs_1_, bf16[1024,768]{1,0:T(8,128)(2,1)} %refs_7_.3, ...), custom_call_target="tpu_custom_call" | custom-call | flops 4831838208 | bytes 9437184 | tf_op jit(solution)/shard_map/pallas_call | solution.py:83
  204.5 12.3 %shard_map.241 = (bf16[1024,768]{1,0:T(8,128)(2,1)}, bf16[1024,768]{1,0:T(8,128)(2,1)}, f32[1,768]{1,0:T(1,128)}, bf16[4,2,96,768]{3,2,1,0:T(8,128)(2,1)}, bf16[...) custom-call(s32[1]{0:T(128)} %bitcast.refs_0_, bf16[1024,768]{1,0:T(8,128)(2,1)} %copy-done.48, bf16[1024,768]{1,0:T(8,128)(2,1)} %refs_7_.3, ...), custom_call_target="tpu_custom_call" | custom-call | flops 4831838208 | bytes 12582912 | tf_op jit(solution)/shard_map/pallas_call | solution.py:83
  228.3 15.7 %shard_map.244 = (f32[1024,768]{1,0:T(8,128)}, f32[1024,768]{1,0:T(8,128)}, f32[5,768]{1,0:T(8,128)}, f32[8,128]{1,0:T(8,128)}) custom-call(s32[1]{0:T(128)} %bitcast.refs_0_, bf16[1024,768]{1,0:T(8,128)(2,1)} %get-tuple-element.209.refs_2_.refs_1_, bf16[1024,768]{1,0:T(8,128)(2,1)} %get-tuple-element.231.refs_2_, ...), custom_call_target="tpu_custom_call" | custom-call | flops 7247757312 | bytes 15728640 | tf_op jit(solution)/shard_map/pallas_call | solution.py:83
  248.6 5.4 %collective-permute-done.17.refs_2_ = bf16[4,96,768]{2,1,0:T(8,128)(2,1)} collective-permute-done((bf16[4,96,768]{2,1,0:T(8,128)(2,1)}, bf16[4,96,768]{2,1,0:T(8,128)(2,1)}, u32[]{:S(2)}, u32[]{:S(2)}) %collective-permute-start.17) | collective-permute-done | bytes 589856 | tf_op jit(solution)/shard_map/ppermute | solution.py:841
  262.8 12.3 %shard_map.247 = (bf16[1024,768]{1,0:T(8,128)(2,1)}, bf16[1024,768]{1,0:T(8,128)(2,1)}, f32[1,768]{1,0:T(1,128)}, bf16[4,2,96,768]{3,2,1,0:T(8,128)(2,1)}, bf16[...) custom-call(s32[1]{0:T(128)} %bitcast.refs_0_, bf16[1024,768]{1,0:T(8,128)(2,1)} %copy-done.48, bf16[1024,768]{1,0:T(8,128)(2,1)} %refs_7_.3, ...), custom_call_target="tpu_custom_call" | custom-call | flops 4831838208 | bytes 12582912 | tf_op jit(solution)/shard_map/pallas_call | solution.py:83
  275.1 7.8 %collective-permute-done.24.refs_1_ = bf16[4,96,768]{2,1,0:T(8,128)(2,1)S(1)} collective-permute-done((bf16[4,96,768]{2,1,0:T(8,128)(2,1)S(1)}, bf16[4,96,768]{2,1,0:T(8,128)(2,1)S(1)}, u32[]{:S(2)}, u32[]{:S(2)}) %collective-permute-start.24) | collective-permute-done | bytes 589856 | tf_op jit(solution)/shard_map/ppermute | solution.py:841
  296.3 10.9 %shard_map.253 = (f32[1024,768]{1,0:T(8,128)}, f32[1024,768]{1,0:T(8,128)}, f32[8,128]{1,0:T(8,128)}) custom-call(s32[1]{0:T(128)} %bitcast.refs_0_, bf16[1024,768]{1,0:T(8,128)(2,1)} %get-tuple-element.240.refs_1_, bf16[1024,768]{1,0:T(8,128)(2,1)} %get-tuple-element.241.refs_2_, bf16[1024,768]{1,0:T(8,128)(2,1)} %get-tuple-element.242.refs_3_, ...), custom_call_target="tpu_custom_call" | custom-call | flops 4831838208 | bytes 12582912 | tf_op jit(solution)/shard_map/pallas_call | solution.py:83
  315.4 12.7 %shard_map.256 = (bf16[1024,768]{1,0:T(8,128)(2,1)}, f32[1024,768]{1,0:T(8,128)}, f32[2,768]{1,0:T(2,128)}, f32[8,128]{1,0:T(8,128)}) custom-call(s32[1]{0:T(128)} %bitcast.refs_0_, bf16[1024,768]{1,0:T(8,128)(2,1)} %get-tuple-element.237.refs_1_, bf16[1024,768]{1,0:T(8,128)(2,1)} %get-tuple-element.238.refs_2_, f32[1024,768]{1,0:T(8,128)} %get-tuple-element.239.refs_3_, ...), custom_call_target="tpu_custom_call" | custom-call | flops 2415919104 | bytes 9437184 | tf_op jit(solution)/shard_map/pallas_call | solution.py:83
  347.1 6.4 %collective-permute-done.33.refs_1_ = bf16[2,96,768]{2,1,0:T(8,128)(2,1)S(1)} collective-permute-done((bf16[2,96,768]{2,1,0:T(8,128)(2,1)S(1)}, bf16[2,96,768]{2,1,0:T(8,128)(2,1)S(1)}, u32[]{:S(2)}, u32[]{:S(2)}) %collective-permute-start.33) | collective-permute-done | bytes 294944 | tf_op jit(solution)/shard_map/ppermute | solution.py:841
  364.7 5.6 %shard_map.267 = (f32[1,1]{1,0:T(1,128)}, f32[13,768]{1,0:T(8,128)}, f32[13,768]{1,0:T(8,128)}, f32[13,768]{1,0:T(8,128)}, f32[13,768]{1,0:T(8,128)}, /*index=5*...) custom-call(s32[3,6]{1,0:T(4,128)S(1)} %pad_add_fusion.src_ref, ...), custom_call_target="tpu_custom_call" | custom-call | flops 8847360 | bytes 14155776 | tf_op jit(solution)/shard_map/pallas_call | solution.py:663
  (252 shorter events, 120.9 us)
Async XLA Ops:
  7.2 92.6 %all-gather.7.cloned.1.call-start = ((), (), s32[]{:S(2)}) async-start(), calls=%async_computation | async-start | bytes 5308416 | tf_op jit(solution)/shard_map/all_gather | solution.py:878
  10.3 17.6 %collective-permute-start = (bf16[4,96,768]{2,1,0:T(8,128)(2,1)S(1)}, bf16[4,96,768]{2,1,0:T(8,128)(2,1)S(1)}, u32[]{:S(2)}, u32[]{:S(2)}) collective-permute-start(bf16[4,96,768]{2,1,0:T(8,128)(2,1)S(1)} %get-tuple-element.167.refs_0_), channel_id=1, source_target_pairs={{0,1},{3,2},{4,5},{7,6},{8,9},{11,10},{12,13},{15,14},{16,17},{19,... | collective-permute-start | bytes 1769480 | tf_op jit(solution)/shard_map/ppermute | solution.py:853
  29.8 18.6 %collective-permute-start.3 = (bf16[4,96,768]{2,1,0:T(8,128)(2,1)S(1)}, bf16[4,96,768]{2,1,0:T(8,128)(2,1)S(1)}, u32[]{:S(2)}, u32[]{:S(2)}) collective-permute-start(bf16[4,96,768]{2,1,0:T(8,128)(2,1)S(1)} %get-tuple-element.173.refs_0_), channel_id=1, source_target_pairs={{0,1},{3,2},{4,5},{7,6},{8,9},{11,10},{12,13},{15,14},{16,17},{19,... | collective-permute-start | bytes 1769480 | tf_op jit(solution)/shard_map/ppermute | solution.py:853
  37.1 22.5 %collective-permute-start.2 = (bf16[4,96,768]{2,1,0:T(8,128)(2,1)S(1)}, bf16[4,96,768]{2,1,0:T(8,128)(2,1)S(1)}, u32[]{:S(2)}, u32[]{:S(2)}) collective-permute-start(bf16[4,96,768]{2,1,0:T(8,128)(2,1)S(1)} %get-tuple-element.172.refs_1_), channel_id=1, source_target_pairs={{1,0},{2,3},{5,4},{6,7},{9,8},{10,11},{13,12},{14,15},{17,16},{18,... | collective-permute-start | bytes 1769480 | tf_op jit(solution)/shard_map/ppermute | solution.py:853
  60.5 82.5 %all-gather.11.cloned.1.call-start = ((), (), s32[]{:S(2)}) async-start(), calls=%async_computation.2 | async-start | bytes 5308416 | tf_op jit(solution)/shard_map/all_gather | solution.py:878
  66.7 19.4 %collective-permute-start.7 = (bf16[4,96,768]{2,1,0:T(8,128)(2,1)S(1)}, bf16[4,96,768]{2,1,0:T(8,128)(2,1)S(1)}, u32[]{:S(2)}, u32[]{:S(2)}) collective-permute-start(bf16[4,96,768]{2,1,0:T(8,128)(2,1)S(1)} %get-tuple-element.182.refs_1_), channel_id=1, source_target_pairs={{1,0},{2,3},{5,4},{6,7},{9,8},{10,11},{13,12},{14,15},{17,16},{18,... | collective-permute-start | bytes 1769480 | tf_op jit(solution)/shard_map/ppermute | solution.py:853
  87.0 117.5 %all-gather.9.cloned.1.call-start = ((), (), s32[]{:S(2)}) async-start(), calls=%async_computation.1 | async-start | bytes 5308416 | tf_op jit(solution)/shard_map/all_gather | solution.py:878
  89.9 34.7 %collective-permute-start.8 = (bf16[4,96,768]{2,1,0:T(8,128)(2,1)}, bf16[4,96,768]{2,1,0:T(8,128)(2,1)}, u32[]{:S(2)}, u32[]{:S(2)}) collective-permute-start(bf16[4,96,768]{2,1,0:T(8,128)(2,1)} %get-tuple-element.185.refs_1_), channel_id=1, source_target_pairs={{1,0},{2,3},{5,4},{6,7},{9,8},{10,11},{13,12},{14,15},{17,16},{18,... | collective-permute-start | bytes 1769480 | tf_op jit(solution)/shard_map/ppermute | solution.py:853
  139.5 45.6 %collective-permute-start.11 = (bf16[4,96,768]{2,1,0:T(8,128)(2,1)}, bf16[4,96,768]{2,1,0:T(8,128)(2,1)S(1)}, u32[]{:S(2)}, u32[]{:S(2)}) collective-permute-start(bf16[4,96,768]{2,1,0:T(8,128)(2,1)} %get-tuple-element.214), channel_id=1, source_target_pairs={{0,8},{4,12},{8,0},{12,4},{16,24},{20,28},{24,16},{28,20},{1,9},{5... | collective-permute-start | bytes 1769480 | tf_op jit(solution)/shard_map/ppermute | solution.py:841
  141.0 44.1 %collective-permute-start.12 = (bf16[4,96,768]{2,1,0:T(8,128)(2,1)}, bf16[4,96,768]{2,1,0:T(8,128)(2,1)S(1)}, u32[]{:S(2)}, u32[]{:S(2)}) collective-permute-start(bf16[4,96,768]{2,1,0:T(8,128)(2,1)} %get-tuple-element.215), channel_id=1, source_target_pairs={{0,16},{4,20},{8,24},{12,28},{16,0},{20,4},{24,8},{28,12},{1,17},{... | collective-permute-start | bytes 1769480 | tf_op jit(solution)/shard_map/ppermute | solution.py:841
  141.8 44.1 %collective-permute-start.13 = (bf16[4,96,768]{2,1,0:T(8,128)(2,1)}, bf16[4,96,768]{2,1,0:T(8,128)(2,1)}, u32[]{:S(2)}, u32[]{:S(2)}) collective-permute-start(bf16[4,96,768]{2,1,0:T(8,128)(2,1)} %get-tuple-element.216), channel_id=1, source_target_pairs={{0,24},{4,28},{8,16},{12,20},{16,8},{20,12},{24,0},{28,4},{1,25},{... | collective-permute-start | bytes 1769480 | tf_op jit(solution)/shard_map/ppermute | solution.py:841
  200.7 18.6 %collective-permute-start.14 = (bf16[4,4,96,768]{3,2,1,0:T(8,128)(2,1)}, bf16[4,4,96,768]{3,2,1,0:T(8,128)(2,1)}, u32[]{:S(2)}, u32[]{:S(2)}) collective-permute-start(bf16[4,4,96,768]{3,2,1,0:T(8,128)(2,1)} %get-tuple-element.220), channel_id=1, source_target_pairs={{0,4},{4,0},{8,12},{12,8},{16,20},{20,16},{24,28},{28,24},{1,5},{5... | collective-permute-start | bytes 7077896 | tf_op jit(solution)/shard_map/ppermute | solution.py:841
  200.8 17.7 %collective-permute-start.15 = (bf16[4,96,768]{2,1,0:T(8,128)(2,1)S(1)}, bf16[4,96,768]{2,1,0:T(8,128)(2,1)S(1)}, u32[]{:S(2)}, u32[]{:S(2)}) collective-permute-start(bf16[4,96,768]{2,1,0:T(8,128)(2,1)S(1)} %get-tuple-element.221.refs_0_), channel_id=1, source_target_pairs={{0,1},{1,0},{2,3},{3,2},{4,5},{5,4},{6,7},{7,6},{8,9},{9,8},{10,11... | collective-permute-start | bytes 1769480 | tf_op jit(solution)/shard_map/ppermute | solution.py:841
  216.8 27.2 %collective-permute-start.19 = (bf16[4,2,96,768]{3,2,1,0:T(8,128)(2,1)}, bf16[4,2,96,768]{3,2,1,0:T(8,128)(2,1)}, u32[]{:S(2)}, u32[]{:S(2)}) collective-permute-start(bf16[4,2,96,768]{3,2,1,0:T(8,128)(2,1)} %get-tuple-element.230), channel_id=1, source_target_pairs={{0,4},{4,0},{8,12},{12,8},{16,20},{20,16},{24,28},{28,24},{1,5},{5... | collective-permute-start | bytes 3538952 | tf_op jit(solution)/shard_map/ppermute | solution.py:841
  224.8 23.8 %collective-permute-start.16 = (bf16[4,96,768]{2,1,0:T(8,128)(2,1)}, bf16[4,96,768]{2,1,0:T(8,128)(2,1)}, u32[]{:S(2)}, u32[]{:S(2)}) collective-permute-start(bf16[4,96,768]{2,1,0:T(8,128)(2,1)} %get-tuple-element.226), channel_id=1, source_target_pairs={{0,8},{4,12},{8,0},{12,4},{16,24},{20,28},{24,16},{28,20},{1,9},{5... | collective-permute-start | bytes 1769480 | tf_op jit(solution)/shard_map/ppermute | solution.py:841
  226.3 27.8 %collective-permute-start.17 = (bf16[4,96,768]{2,1,0:T(8,128)(2,1)}, bf16[4,96,768]{2,1,0:T(8,128)(2,1)}, u32[]{:S(2)}, u32[]{:S(2)}) collective-permute-start(bf16[4,96,768]{2,1,0:T(8,128)(2,1)} %get-tuple-element.227), channel_id=1, source_target_pairs={{0,16},{4,20},{8,24},{12,28},{16,0},{20,4},{24,8},{28,12},{1,17},{... | collective-permute-start | bytes 1769480 | tf_op jit(solution)/shard_map/ppermute | solution.py:841
  227.9 26.1 %collective-permute-start.18 = (bf16[4,96,768]{2,1,0:T(8,128)(2,1)}, bf16[4,96,768]{2,1,0:T(8,128)(2,1)}, u32[]{:S(2)}, u32[]{:S(2)}) collective-permute-start(bf16[4,96,768]{2,1,0:T(8,128)(2,1)} %get-tuple-element.228), channel_id=1, source_target_pairs={{0,24},{4,28},{8,16},{12,20},{16,8},{20,12},{24,0},{28,4},{1,25},{... | collective-permute-start | bytes 1769480 | tf_op jit(solution)/shard_map/ppermute | solution.py:841
  256.4 26.5 %collective-permute-start.24 = (bf16[4,96,768]{2,1,0:T(8,128)(2,1)S(1)}, bf16[4,96,768]{2,1,0:T(8,128)(2,1)S(1)}, u32[]{:S(2)}, u32[]{:S(2)}) collective-permute-start(bf16[4,96,768]{2,1,0:T(8,128)(2,1)S(1)} %get-tuple-element.251.refs_0_), channel_id=1, source_target_pairs={{0,1},{1,0},{2,3},{3,2},{4,5},{5,4},{6,7},{7,6},{8,9},{9,8},{10,11... | collective-permute-start | bytes 1769480 | tf_op jit(solution)/shard_map/ppermute | solution.py:841
  257.9 27.6 %collective-permute-start.23 = (bf16[4,96,768]{2,1,0:T(8,128)(2,1)S(1)}, bf16[4,96,768]{2,1,0:T(8,128)(2,1)S(1)}, u32[]{:S(2)}, u32[]{:S(2)}) collective-permute-start(bf16[4,96,768]{2,1,0:T(8,128)(2,1)S(1)} %get-tuple-element.250.refs_0_), channel_id=1, source_target_pairs={{0,2},{1,3},{2,0},{3,1},{4,6},{5,7},{6,4},{7,5},{8,10},{9,11},{10,... | collective-permute-start | bytes 1769480 | tf_op jit(solution)/shard_map/ppermute | solution.py:841
  259.3 27.2 %collective-permute-start.20 = (bf16[2,96,768]{2,1,0:T(8,128)(2,1)}, bf16[2,96,768]{2,1,0:T(8,128)(2,1)}, u32[]{:S(2)}, u32[]{:S(2)}) collective-permute-start(bf16[2,96,768]{2,1,0:T(8,128)(2,1)} %get-tuple-element.247), channel_id=1, source_target_pairs={{0,8},{4,12},{8,0},{12,4},{16,24},{20,28},{24,16},{28,20},{1,9},{5... | collective-permute-start | bytes 884744 | tf_op jit(solution)/shard_map/ppermute | solution.py:841
  260.7 25.8 %collective-permute-start.21 = (bf16[2,96,768]{2,1,0:T(8,128)(2,1)}, bf16[2,96,768]{2,1,0:T(8,128)(2,1)}, u32[]{:S(2)}, u32[]{:S(2)}) collective-permute-start(bf16[2,96,768]{2,1,0:T(8,128)(2,1)} %get-tuple-element.248), channel_id=1, source_target_pairs={{0,16},{4,20},{8,24},{12,28},{16,0},{20,4},{24,8},{28,12},{1,17},{... | collective-permute-start | bytes 884744 | tf_op jit(solution)/shard_map/ppermute | solution.py:841
  261.4 25.1 %collective-permute-start.22 = (bf16[2,96,768]{2,1,0:T(8,128)(2,1)}, bf16[2,96,768]{2,1,0:T(8,128)(2,1)}, u32[]{:S(2)}, u32[]{:S(2)}) collective-permute-start(bf16[2,96,768]{2,1,0:T(8,128)(2,1)} %get-tuple-element.249), channel_id=1, source_target_pairs={{0,24},{4,28},{8,16},{12,20},{16,8},{20,12},{24,0},{28,4},{1,25},{... | collective-permute-start | bytes 884744 | tf_op jit(solution)/shard_map/ppermute | solution.py:841
  288.1 24.6 %collective-permute-start.26 = (bf16[2,96,768]{2,1,0:T(8,128)(2,1)S(1)}, bf16[2,96,768]{2,1,0:T(8,128)(2,1)S(1)}, u32[]{:S(2)}, u32[]{:S(2)}) collective-permute-start(bf16[2,96,768]{2,1,0:T(8,128)(2,1)S(1)} %get-tuple-element.262.refs_0_), channel_id=1, source_target_pairs={{0,1},{1,0},{2,3},{3,2},{4,5},{5,4},{6,7},{7,6},{8,9},{9,8},{10,11... | collective-permute-start | bytes 884744 | tf_op jit(solution)/shard_map/ppermute | solution.py:841
  288.2 43.3 %collective-permute-start.30 = (bf16[4,96,768]{2,1,0:T(8,128)(2,1)S(1)}, bf16[4,96,768]{2,1,0:T(8,128)(2,1)S(1)}, u32[]{:S(2)}, u32[]{:S(2)}) collective-permute-start(bf16[4,96,768]{2,1,0:T(8,128)(2,1)S(1)} %get-tuple-element.273.refs_0_), channel_id=1, source_target_pairs={{0,2},{1,3},{2,0},{3,1},{4,6},{5,7},{6,4},{7,5},{8,10},{9,11},{10,... | collective-permute-start | bytes 1769480 | tf_op jit(solution)/shard_map/ppermute | solution.py:841
  (80 other events, 620.9 us)
Sparse Core Ops, SparseCore 0:
  60.7 39.0 all-gather.6
  101.6 38.9 all-gather.10
  143.0 55.6 all-gather.8

commit v2 on v1

--- a/solution.py
+++ b/solution.py
@@ -485,7 +485,7 @@
     )(me, h_one, a, cot, *dqkv, *deps)
 
 
-def products(me, jobs, tail, outs, starts=None, extra=(), deps=(), mib=60):
+def products(me, jobs, tail, outs, starts=None, extra=(), deps=(), mib=48):
     starts = starts or [()] * len(jobs)
     rows = jobs[0][0][0].shape[0]
     tile = 256

time: 382 us -> 370 us (0.969)
  local copies, waits for them, and re-layouts: 29.9 us -> 16.3 us
  waiting for transfers between devices: 95.6 us -> 108 us
  Pallas kernels: 179 us -> 169 us
    unnamed x118 -> x98, local copies, waits for them, and re-layouts: 28.1 us -> 14.5 us
    ppermute x33, waiting for transfers between devices: 38.6 us -> 50.6 us  [swap(): return lax.ppermute(value, axis, [(i, i ^ bit) for i in range(size)])]
    pallas_call x47, Pallas kernels: 173 us -> 163 us  [run(): *out, token = call(*args, *deps)]
  transfers between devices with their start and end apart: 45 -> 45, of which waited for: 22 -> 21; matrix products, arithmetic and copies ran while one was open for 1% -> 1% of each run, Pallas kernels for 44% -> 43%
where the time goes in v2:
time: 370 us; the launch traced here: 366 us
  Pallas kernels  169 us (46%)
  waiting for transfers between devices  108 us (29%)
  starting transfers between devices  54.9 us (15%)
  local copies, waits for them, and re-layouts  16.3 us (4%)
  between operations  15.6 us (4%)
    pallas_call x47, Pallas kernels, run(): *out, token = call(*args, *deps)  163 us
    ppermute x33, waiting for transfers between devices, swap(): return lax.ppermute(value, axis, [(i, i ^ bit) for i in range(size)])  50.6 us
    ppermute x9, waiting for transfers between devices, hop(): return lax.ppermute(value, 'narrow', pairs)  48.8 us
    ppermute x33, starting transfers between devices, swap(): return lax.ppermute(value, axis, [(i, i ^ bit) for i in range(size)])  32.1 us
    ppermute x9, starting transfers between devices, hop(): return lax.ppermute(value, 'narrow', pairs)  22.7 us
    unnamed x98, local copies, waits for them, and re-layouts  14.5 us
    all_gather x3, waiting for transfers between devices, gather_wide(): full = lax.all_gather(value, 'wide', axis=0, tiled=False)  8.96 us
  transfers between devices with their start and end apart: 45, of which 21 were waited for; matrix products, arithmetic and copies ran while one was open for 1% of the time, Pallas kernels for 43%

profile of v2, /device:TPU:0, one launch (start us, length us, event | category | flops | bytes accessed | tf_op | source)
XLA Modules:
  0.0 365.7 jit_solution(16024886336064499838)
XLA Ops:
  10.3 5.1 %collective-permute-start = (bf16[4,96,768]{2,1,0:T(8,128)(2,1)S(1)}, bf16[4,96,768]{2,1,0:T(8,128)(2,1)S(1)}, u32[]{:S(2)}, u32[]{:S(2)}) collective-permute-start(bf16[4,96,768]{2,1,0:T(8,128)(2,1)S(1)} %get-tuple-element.167.refs_0_), channel_id=1, source_target_pairs={{0,1},{3,2},{4,5},{7,6},{8,9},{11,10},{12,13},{15,14},{16,17},{19,... | collective-permute-start | bytes 1769480 | tf_op jit(solution)/shard_map/ppermute | solution.py:853
  18.2 9.8 %collective-permute-done.refs_1_ = bf16[4,96,768]{2,1,0:T(8,128)(2,1)S(1)} collective-permute-done((bf16[4,96,768]{2,1,0:T(8,128)(2,1)S(1)}, bf16[4,96,768]{2,1,0:T(8,128)(2,1)S(1)}, u32[]{:S(2)}, u32[]{:S(2)}) %collective-permute-start) | collective-permute-done | bytes 589856 | tf_op jit(solution)/shard_map/ppermute | solution.py:853
  29.8 7.2 %collective-permute-start.3 = (bf16[4,96,768]{2,1,0:T(8,128)(2,1)S(1)}, bf16[4,96,768]{2,1,0:T(8,128)(2,1)S(1)}, u32[]{:S(2)}, u32[]{:S(2)}) collective-permute-start(bf16[4,96,768]{2,1,0:T(8,128)(2,1)S(1)} %get-tuple-element.173.refs_0_), channel_id=1, source_target_pairs={{0,1},{3,2},{4,5},{7,6},{8,9},{11,10},{12,13},{15,14},{16,17},{19,... | collective-permute-start | bytes 1769480 | tf_op jit(solution)/shard_map/ppermute | solution.py:853
  38.4 9.9 %collective-permute-done.3.refs_1_ = bf16[4,96,768]{2,1,0:T(8,128)(2,1)S(1)} collective-permute-done((bf16[4,96,768]{2,1,0:T(8,128)(2,1)S(1)}, bf16[4,96,768]{2,1,0:T(8,128)(2,1)S(1)}, u32[]{:S(2)}, u32[]{:S(2)}) %collective-permute-start.3) | collective-permute-done | bytes 589856 | tf_op jit(solution)/shard_map/ppermute | solution.py:853
  48.5 11.1 %collective-permute-done.2.refs_2_ = bf16[4,96,768]{2,1,0:T(8,128)(2,1)S(1)} collective-permute-done((bf16[4,96,768]{2,1,0:T(8,128)(2,1)S(1)}, bf16[4,96,768]{2,1,0:T(8,128)(2,1)S(1)}, u32[]{:S(2)}, u32[]{:S(2)}) %collective-permute-start.2) | collective-permute-done | bytes 589856 | tf_op jit(solution)/shard_map/ppermute | solution.py:853
  68.0 8.4 %collective-permute-done.4.refs_1_ = bf16[4,96,768]{2,1,0:T(8,128)(2,1)S(1)} collective-permute-done((bf16[4,96,768]{2,1,0:T(8,128)(2,1)S(1)}, bf16[4,96,768]{2,1,0:T(8,128)(2,1)S(1)}, u32[]{:S(2)}, u32[]{:S(2)}) %collective-permute-start.4) | collective-permute-done | bytes 589856 | tf_op jit(solution)/shard_map/ppermute | solution.py:853
  76.5 9.6 %collective-permute-done.7.refs_2_ = bf16[4,96,768]{2,1,0:T(8,128)(2,1)S(1)} collective-permute-done((bf16[4,96,768]{2,1,0:T(8,128)(2,1)S(1)}, bf16[4,96,768]{2,1,0:T(8,128)(2,1)S(1)}, u32[]{:S(2)}, u32[]{:S(2)}) %collective-permute-start.7) | collective-permute-done | bytes 589856 | tf_op jit(solution)/shard_map/ppermute | solution.py:853
  90.8 9.0 %all-gather.7.cloned.1.call-done = bf16[32,96,768]{2,1,0:T(8,128)(2,1)} async-done(((bf16[4,96,768]{2,1,0:T(8,128)(2,1)}), bf16[32,96,768]{2,1,0:T(8,128)(2,1)}) %all-gather.7.cloned.1.call-update) | async-done | bytes 4718608 | tf_op jit(solution)/shard_map/all_gather | solution.py:878
  99.7 12.3 %shard_map.232 = (bf16[1024,768]{1,0:T(8,128)(2,1)}, bf16[1024,768]{1,0:T(8,128)(2,1)}, f32[1,768]{1,0:T(1,128)}, bf16[4,2,96,768]{3,2,1,0:T(8,128)(2,1)}, bf16[...) custom-call(s32[1]{0:T(128)} %bitcast.refs_0_, bf16[1024,768]{1,0:T(8,128)(2,1)} %copy-done.34, bf16[1024,768]{1,0:T(8,128)(2,1)} %refs_7_.3, ...), custom_call_target="tpu_custom_call" | custom-call | flops 4831838208 | bytes 12582912 | tf_op jit(solution)/shard_map/pallas_call | solution.py:83
  112.0 12.6 %shard_map.233 = (bf16[1024,768]{1,0:T(8,128)(2,1)}, bf16[1024,768]{1,0:T(8,128)(2,1)}, f32[1,768]{1,0:T(1,128)}, bf16[4,2,96,768]{3,2,1,0:T(8,128)(2,1)}, bf16[...) custom-call(s32[1]{0:T(128)} %bitcast.refs_0_, bf16[1024,768]{1,0:T(8,128)(2,1)} %copy-done.34, bf16[1024,768]{1,0:T(8,128)(2,1)} %refs_7_.3, ...), custom_call_target="tpu_custom_call" | custom-call | flops 4831838208 | bytes 12582912 | tf_op jit(solution)/shard_map/pallas_call | solution.py:83
  143.0 12.3 %shard_map.236 = (bf16[1024,768]{1,0:T(8,128)(2,1)}, bf16[1024,768]{1,0:T(8,128)(2,1)}, bf16[1024,768]{1,0:T(8,128)(2,1)}, bf16[1024,768]{1,0:T(8,128)(2,1)}, f32[8,128]{1,0:T(8,128)}) custom-call(s32[1]{0:T(128)} %bitcast.refs_0_, bf16[1024,768]{1,0:T(8,128)(2,1)} %copy-done.35, bf16[1024,768]{1,0:T(8,128)(2,1)} %refs_7_.3, f32[3,768]{1,0:T(4,128)} %slice.18.refs_3_, ...), custom_call_target="tpu_custom_call" | custom-call | flops 4831838208 | bytes 15728640 | tf_op jit(solution)/shard_map/pallas_call | solution.py:83
  155.3 14.6 %shard_map.237 = (bf16[1024,768]{1,0:T(8,128)(2,1)}, bf16[1024,768]{1,0:T(8,128)(2,1)}, bf16[1024,768]{1,0:T(8,128)(2,1)}, bf16[1024,768]{1,0:T(8,128)(2,1)}, f32[1,3,768]{2,1,0:T(4,128)}, /*index=5*/f32[8,128]{1,0:T(8,128)}) custom-call(bf16[1024,768]{1,0:T(8,128)(2,1)} %get-tuple-element.199.refs_0_, bf16[1024,768]{1,0:T(8,128)(2,1)} %get-tuple-element.200.refs_1_, ...), custom_call_target="tpu_custom_call" | custom-call | flops 10000000000 | bytes 15728640 | tf_op jit(solution)/shard_map/pallas_call | solution.py:83
  169.9 15.1 %shard_map.238 = (bf16[1024,768]{1,0:T(8,128)(2,1)}, bf16[1024,768]{1,0:T(8,128)(2,1)}, bf16[1024,768]{1,0:T(8,128)(2,1)}, bf16[1024,768]{1,0:T(8,128)(2,1)}, f32[1,3,768]{2,1,0:T(4,128)}, /*index=5*/f32[8,128]{1,0:T(8,128)}) custom-call(bf16[1024,768]{1,0:T(8,128)(2,1)} %get-tuple-element.199, ...), custom_call_target="tpu_custom_call", output_to_operand_aliasing={{0}: (7, {}), {1}: (8, {}), {2}: (9, {}), {3}: (10, {})} | custom-call | flops 10000000000 | bytes 15728640 | tf_op jit(solution)/shard_map/pallas_call | solution.py:83
  189.5 11.0 %shard_map.240 = (bf16[4,4,96,768]{3,2,1,0:T(8,128)(2,1)}, bf16[4,4,96,768]{3,2,1,0:T(8,128)(2,1)}, f32[8,128]{1,0:T(8,128)}) custom-call(s32[1]{0:T(128)} %bitcast.refs_0_, bf16[1024,768]{1,0:T(8,128)(2,1)} %copy-done.35, bf16[1024,768]{1,0:T(8,128)(2,1)} %get-tuple-element.209.refs_2_.refs_1_, bf16[1024,768]{1,0:T(8,128)(2,1)} %refs_7_.3, ...), custom_call_target="tpu_custom_call" | custom-call | flops 4831838208 | bytes 9437184 | tf_op jit(solution)/shard_map/pallas_call | solution.py:83
  203.6 12.3 %shard_map.241 = (bf16[1024,768]{1,0:T(8,128)(2,1)}, bf16[1024,768]{1,0:T(8,128)(2,1)}, f32[1,768]{1,0:T(1,128)}, bf16[4,2,96,768]{3,2,1,0:T(8,128)(2,1)}, bf16[...) custom-call(s32[1]{0:T(128)} %bitcast.refs_0_, bf16[1024,768]{1,0:T(8,128)(2,1)} %copy-done.34, bf16[1024,768]{1,0:T(8,128)(2,1)} %refs_7_.3, ...), custom_call_target="tpu_custom_call" | custom-call | flops 4831838208 | bytes 12582912 | tf_op jit(solution)/shard_map/pallas_call | solution.py:83
  226.8 14.9 %shard_map.244 = (f32[1024,768]{1,0:T(8,128)}, f32[1024,768]{1,0:T(8,128)}, f32[5,768]{1,0:T(8,128)S(1)}, f32[8,128]{1,0:T(8,128)S(1)}) custom-call(s32[1]{0:T(128)} %bitcast.refs_0_, bf16[1024,768]{1,0:T(8,128)(2,1)S(1)} %copy-done.41, bf16[1024,768]{1,0:T(8,128)(2,1)S(1)} %copy-done.40, bf16[1024,768]{1,0:T(8,128)(2,1)S(1)} %copy-done.42, ...), custom_call_target="tpu_custom_call" | custom-call | flops 7247757312 | bytes 15728640 | tf_op jit(solution)/shard_map/pallas_call | solution.py:83
  243.1 9.1 %collective-permute-done.17.refs_2_ = bf16[4,96,768]{2,1,0:T(8,128)(2,1)S(1)} collective-permute-done((bf16[4,96,768]{2,1,0:T(8,128)(2,1)S(1)}, bf16[4,96,768]{2,1,0:T(8,128)(2,1)S(1)}, u32[]{:S(2)}, u32[]{:S(2)}) %collective-permute-start.17) | collective-permute-done | bytes 589856 | tf_op jit(solution)/shard_map/ppermute | solution.py:841
  259.5 12.4 %shard_map.247 = (bf16[1024,768]{1,0:T(8,128)(2,1)}, bf16[1024,768]{1,0:T(8,128)(2,1)}, f32[1,768]{1,0:T(1,128)}, bf16[4,2,96,768]{3,2,1,0:T(8,128)(2,1)}, bf16[...) custom-call(s32[1]{0:T(128)} %bitcast.refs_0_, bf16[1024,768]{1,0:T(8,128)(2,1)} %copy-done.34, bf16[1024,768]{1,0:T(8,128)(2,1)} %refs_7_.3, ...), custom_call_target="tpu_custom_call" | custom-call | flops 4831838208 | bytes 12582912 | tf_op jit(solution)/shard_map/pallas_call | solution.py:83
  272.0 7.7 %collective-permute-done.24.refs_1_ = bf16[4,96,768]{2,1,0:T(8,128)(2,1)} collective-permute-done((bf16[4,96,768]{2,1,0:T(8,128)(2,1)S(1)}, bf16[4,96,768]{2,1,0:T(8,128)(2,1)}, u32[]{:S(2)}, u32[]{:S(2)}) %collective-permute-start.24) | collective-permute-done | bytes 589856 | tf_op jit(solution)/shard_map/ppermute | solution.py:841
  290.7 10.4 %shard_map.253 = (f32[1024,768]{1,0:T(8,128)}, f32[1024,768]{1,0:T(8,128)}, f32[8,128]{1,0:T(8,128)S(1)}) custom-call(s32[1]{0:T(128)} %bitcast.refs_0_, bf16[1024,768]{1,0:T(8,128)(2,1)S(1)} %copy-done.43, bf16[1024,768]{1,0:T(8,128)(2,1)S(1)} %copy-done.45, bf16[1024,768]{1,0:T(8,128)(2,1)S(1)} %copy-done.44, ...), custom_call_target="tpu_custom_call" | custom-call | flops 4831838208 | bytes 12582912 | tf_op jit(solution)/shard_map/pallas_call | solution.py:83
  306.8 11.3 %shard_map.256 = (bf16[1024,768]{1,0:T(8,128)(2,1)}, f32[1024,768]{1,0:T(8,128)}, f32[2,768]{1,0:T(2,128)S(1)}, f32[8,128]{1,0:T(8,128)S(1)}) custom-call(s32[1]{0:T(128)} %bitcast.refs_0_, bf16[1024,768]{1,0:T(8,128)(2,1)S(1)} %copy-done.7, bf16[1024,768]{1,0:T(8,128)(2,1)S(1)} %copy-done.8, f32[1024,768]{1,0:T(8,128)} %get-tuple-element.239.refs_3_, ...), custom_call_target="tpu_custom_call" | custom-call | flops 2415919104 | bytes 9437184 | tf_op jit(solution)/shard_map/pallas_call | solution.py:83
  318.3 7.4 %collective-permute-done.31.refs_1_ = bf16[2,96,768]{2,1,0:T(8,128)(2,1)S(1)} collective-permute-done((bf16[2,96,768]{2,1,0:T(8,128)(2,1)S(1)}, bf16[2,96,768]{2,1,0:T(8,128)(2,1)S(1)}, u32[]{:S(2)}, u32[]{:S(2)}) %collective-permute-start.31) | collective-permute-done | bytes 294944 | tf_op jit(solution)/shard_map/ppermute | solution.py:841
  336.0 6.7 %collective-permute-done.33.refs_1_ = bf16[2,96,768]{2,1,0:T(8,128)(2,1)S(1)} collective-permute-done((bf16[2,96,768]{2,1,0:T(8,128)(2,1)S(1)}, bf16[2,96,768]{2,1,0:T(8,128)(2,1)S(1)}, u32[]{:S(2)}, u32[]{:S(2)}) %collective-permute-start.33) | collective-permute-done | bytes 294944 | tf_op jit(solution)/shard_map/ppermute | solution.py:841
  353.3 5.6 %shard_map.267 = (f32[1,1]{1,0:T(1,128)}, f32[13,768]{1,0:T(8,128)}, f32[13,768]{1,0:T(8,128)}, f32[13,768]{1,0:T(8,128)}, f32[13,768]{1,0:T(8,128)}, /*index=5*...) custom-call(s32[3,6]{1,0:T(4,128)S(1)} %pad_add_fusion.src_ref, ...), custom_call_target="tpu_custom_call" | custom-call | flops 8847360 | bytes 14155776 | tf_op jit(solution)/shard_map/pallas_call | solution.py:663
  (232 shorter events, 104.4 us)
Async XLA Ops:
  7.2 92.6 %all-gather.7.cloned.1.call-start = ((), (), s32[]{:S(2)}) async-start(), calls=%async_computation | async-start | bytes 5308416 | tf_op jit(solution)/shard_map/all_gather | solution.py:878
  10.3 17.6 %collective-permute-start = (bf16[4,96,768]{2,1,0:T(8,128)(2,1)S(1)}, bf16[4,96,768]{2,1,0:T(8,128)(2,1)S(1)}, u32[]{:S(2)}, u32[]{:S(2)}) collective-permute-start(bf16[4,96,768]{2,1,0:T(8,128)(2,1)S(1)} %get-tuple-element.167.refs_0_), channel_id=1, source_target_pairs={{0,1},{3,2},{4,5},{7,6},{8,9},{11,10},{12,13},{15,14},{16,17},{19,... | collective-permute-start | bytes 1769480 | tf_op jit(solution)/shard_map/ppermute | solution.py:853
  29.8 18.6 %collective-permute-start.3 = (bf16[4,96,768]{2,1,0:T(8,128)(2,1)S(1)}, bf16[4,96,768]{2,1,0:T(8,128)(2,1)S(1)}, u32[]{:S(2)}, u32[]{:S(2)}) collective-permute-start(bf16[4,96,768]{2,1,0:T(8,128)(2,1)S(1)} %get-tuple-element.173.refs_0_), channel_id=1, source_target_pairs={{0,1},{3,2},{4,5},{7,6},{8,9},{11,10},{12,13},{15,14},{16,17},{19,... | collective-permute-start | bytes 1769480 | tf_op jit(solution)/shard_map/ppermute | solution.py:853
  37.1 22.5 %collective-permute-start.2 = (bf16[4,96,768]{2,1,0:T(8,128)(2,1)S(1)}, bf16[4,96,768]{2,1,0:T(8,128)(2,1)S(1)}, u32[]{:S(2)}, u32[]{:S(2)}) collective-permute-start(bf16[4,96,768]{2,1,0:T(8,128)(2,1)S(1)} %get-tuple-element.172.refs_1_), channel_id=1, source_target_pairs={{1,0},{2,3},{5,4},{6,7},{9,8},{10,11},{13,12},{14,15},{17,16},{18,... | collective-permute-start | bytes 1769480 | tf_op jit(solution)/shard_map/ppermute | solution.py:853
  60.5 82.4 %all-gather.11.cloned.1.call-start = ((), (), s32[]{:S(2)}) async-start(), calls=%async_computation.2 | async-start | bytes 5308416 | tf_op jit(solution)/shard_map/all_gather | solution.py:878
  66.7 19.4 %collective-permute-start.7 = (bf16[4,96,768]{2,1,0:T(8,128)(2,1)S(1)}, bf16[4,96,768]{2,1,0:T(8,128)(2,1)S(1)}, u32[]{:S(2)}, u32[]{:S(2)}) collective-permute-start(bf16[4,96,768]{2,1,0:T(8,128)(2,1)S(1)} %get-tuple-element.182.refs_1_), channel_id=1, source_target_pairs={{1,0},{2,3},{5,4},{6,7},{9,8},{10,11},{13,12},{14,15},{17,16},{18,... | collective-permute-start | bytes 1769480 | tf_op jit(solution)/shard_map/ppermute | solution.py:853
  86.9 116.7 %all-gather.9.cloned.1.call-start = ((), (), s32[]{:S(2)}) async-start(), calls=%async_computation.1 | async-start | bytes 5308416 | tf_op jit(solution)/shard_map/all_gather | solution.py:878
  89.3 35.4 %collective-permute-start.8 = (bf16[4,96,768]{2,1,0:T(8,128)(2,1)}, bf16[4,96,768]{2,1,0:T(8,128)(2,1)}, u32[]{:S(2)}, u32[]{:S(2)}) collective-permute-start(bf16[4,96,768]{2,1,0:T(8,128)(2,1)} %get-tuple-element.185.refs_1_), channel_id=1, source_target_pairs={{1,0},{2,3},{5,4},{6,7},{9,8},{10,11},{13,12},{14,15},{17,16},{18,... | collective-permute-start | bytes 1769480 | tf_op jit(solution)/shard_map/ppermute | solution.py:853
  139.5 45.5 %collective-permute-start.11 = (bf16[4,96,768]{2,1,0:T(8,128)(2,1)}, bf16[4,96,768]{2,1,0:T(8,128)(2,1)S(1)}, u32[]{:S(2)}, u32[]{:S(2)}) collective-permute-start(bf16[4,96,768]{2,1,0:T(8,128)(2,1)} %get-tuple-element.214), channel_id=1, source_target_pairs={{0,8},{4,12},{8,0},{12,4},{16,24},{20,28},{24,16},{28,20},{1,9},{5... | collective-permute-start | bytes 1769480 | tf_op jit(solution)/shard_map/ppermute | solution.py:841
  140.9 44.1 %collective-permute-start.12 = (bf16[4,96,768]{2,1,0:T(8,128)(2,1)}, bf16[4,96,768]{2,1,0:T(8,128)(2,1)S(1)}, u32[]{:S(2)}, u32[]{:S(2)}) collective-permute-start(bf16[4,96,768]{2,1,0:T(8,128)(2,1)} %get-tuple-element.215), channel_id=1, source_target_pairs={{0,16},{4,20},{8,24},{12,28},{16,0},{20,4},{24,8},{28,12},{1,17},{... | collective-permute-start | bytes 1769480 | tf_op jit(solution)/shard_map/ppermute | solution.py:841
  141.8 44.0 %collective-permute-start.13 = (bf16[4,96,768]{2,1,0:T(8,128)(2,1)}, bf16[4,96,768]{2,1,0:T(8,128)(2,1)}, u32[]{:S(2)}, u32[]{:S(2)}) collective-permute-start(bf16[4,96,768]{2,1,0:T(8,128)(2,1)} %get-tuple-element.216), channel_id=1, source_target_pairs={{0,24},{4,28},{8,16},{12,20},{16,8},{20,12},{24,0},{28,4},{1,25},{... | collective-permute-start | bytes 1769480 | tf_op jit(solution)/shard_map/ppermute | solution.py:841
  200.5 17.9 %collective-permute-start.14 = (bf16[4,4,96,768]{3,2,1,0:T(8,128)(2,1)}, bf16[4,4,96,768]{3,2,1,0:T(8,128)(2,1)}, u32[]{:S(2)}, u32[]{:S(2)}) collective-permute-start(bf16[4,4,96,768]{3,2,1,0:T(8,128)(2,1)} %get-tuple-element.220), channel_id=1, source_target_pairs={{0,4},{4,0},{8,12},{12,8},{16,20},{20,16},{24,28},{28,24},{1,5},{5... | collective-permute-start | bytes 7077896 | tf_op jit(solution)/shard_map/ppermute | solution.py:841
  215.9 25.8 %collective-permute-start.19 = (bf16[4,2,96,768]{3,2,1,0:T(8,128)(2,1)}, bf16[4,2,96,768]{3,2,1,0:T(8,128)(2,1)S(1)}, u32[]{:S(2)}, u32[]{:S(2)}) collective-permute-start(bf16[4,2,96,768]{3,2,1,0:T(8,128)(2,1)} %get-tuple-element.230), channel_id=1, source_target_pairs={{0,4},{4,0},{8,12},{12,8},{16,20},{20,16},{24,28},{28,24},{1,5},{5... | collective-permute-start | bytes 3538952 | tf_op jit(solution)/shard_map/ppermute | solution.py:841
  223.2 19.8 %collective-permute-start.16 = (bf16[4,96,768]{2,1,0:T(8,128)(2,1)S(1)}, bf16[4,96,768]{2,1,0:T(8,128)(2,1)S(1)}, u32[]{:S(2)}, u32[]{:S(2)}) collective-permute-start(bf16[4,96,768]{2,1,0:T(8,128)(2,1)S(1)} %get-tuple-element.226), channel_id=1, source_target_pairs={{0,8},{4,12},{8,0},{12,4},{16,24},{20,28},{24,16},{28,20},{1,9},{5... | collective-permute-start | bytes 1769480 | tf_op jit(solution)/shard_map/ppermute | solution.py:841
  224.8 27.4 %collective-permute-start.17 = (bf16[4,96,768]{2,1,0:T(8,128)(2,1)S(1)}, bf16[4,96,768]{2,1,0:T(8,128)(2,1)S(1)}, u32[]{:S(2)}, u32[]{:S(2)}) collective-permute-start(bf16[4,96,768]{2,1,0:T(8,128)(2,1)S(1)} %get-tuple-element.227), channel_id=1, source_target_pairs={{0,16},{4,20},{8,24},{12,28},{16,0},{20,4},{24,8},{28,12},{1,17},{... | collective-permute-start | bytes 1769480 | tf_op jit(solution)/shard_map/ppermute | solution.py:841
  226.2 26.0 %collective-permute-start.18 = (bf16[4,96,768]{2,1,0:T(8,128)(2,1)S(1)}, bf16[4,96,768]{2,1,0:T(8,128)(2,1)S(1)}, u32[]{:S(2)}, u32[]{:S(2)}) collective-permute-start(bf16[4,96,768]{2,1,0:T(8,128)(2,1)S(1)} %get-tuple-element.228), channel_id=1, source_target_pairs={{0,24},{4,28},{8,16},{12,20},{16,8},{20,12},{24,0},{28,4},{1,25},{... | collective-permute-start | bytes 1769480 | tf_op jit(solution)/shard_map/ppermute | solution.py:841
  253.1 26.6 %collective-permute-start.24 = (bf16[4,96,768]{2,1,0:T(8,128)(2,1)S(1)}, bf16[4,96,768]{2,1,0:T(8,128)(2,1)}, u32[]{:S(2)}, u32[]{:S(2)}) collective-permute-start(bf16[4,96,768]{2,1,0:T(8,128)(2,1)S(1)} %get-tuple-element.251.refs_0_), channel_id=1, source_target_pairs={{0,1},{1,0},{2,3},{3,2},{4,5},{5,4},{6,7},{7,6},{8,9},{9,8},{10,11... | collective-permute-start | bytes 1769480 | tf_op jit(solution)/shard_map/ppermute | solution.py:841
  254.7 27.0 %collective-permute-start.23 = (bf16[4,96,768]{2,1,0:T(8,128)(2,1)S(1)}, bf16[4,96,768]{2,1,0:T(8,128)(2,1)S(1)}, u32[]{:S(2)}, u32[]{:S(2)}) collective-permute-start(bf16[4,96,768]{2,1,0:T(8,128)(2,1)S(1)} %get-tuple-element.250.refs_0_), channel_id=1, source_target_pairs={{0,2},{1,3},{2,0},{3,1},{4,6},{5,7},{6,4},{7,5},{8,10},{9,11},{10,... | collective-permute-start | bytes 1769480 | tf_op jit(solution)/shard_map/ppermute | solution.py:841
  256.1 26.0 %collective-permute-start.20 = (bf16[2,96,768]{2,1,0:T(8,128)(2,1)}, bf16[2,96,768]{2,1,0:T(8,128)(2,1)}, u32[]{:S(2)}, u32[]{:S(2)}) collective-permute-start(bf16[2,96,768]{2,1,0:T(8,128)(2,1)} %get-tuple-element.247), channel_id=1, source_target_pairs={{0,8},{4,12},{8,0},{12,4},{16,24},{20,28},{24,16},{28,20},{1,9},{5... | collective-permute-start | bytes 884744 | tf_op jit(solution)/shard_map/ppermute | solution.py:841
  257.3 24.7 %collective-permute-start.21 = (bf16[2,96,768]{2,1,0:T(8,128)(2,1)}, bf16[2,96,768]{2,1,0:T(8,128)(2,1)}, u32[]{:S(2)}, u32[]{:S(2)}) collective-permute-start(bf16[2,96,768]{2,1,0:T(8,128)(2,1)} %get-tuple-element.248), channel_id=1, source_target_pairs={{0,16},{4,20},{8,24},{12,28},{16,0},{20,4},{24,8},{28,12},{1,17},{... | collective-permute-start | bytes 884744 | tf_op jit(solution)/shard_map/ppermute | solution.py:841
  258.1 23.9 %collective-permute-start.22 = (bf16[2,96,768]{2,1,0:T(8,128)(2,1)}, bf16[2,96,768]{2,1,0:T(8,128)(2,1)}, u32[]{:S(2)}, u32[]{:S(2)}) collective-permute-start(bf16[2,96,768]{2,1,0:T(8,128)(2,1)} %get-tuple-element.249), channel_id=1, source_target_pairs={{0,24},{4,28},{8,16},{12,20},{16,8},{20,12},{24,0},{28,4},{1,25},{... | collective-permute-start | bytes 884744 | tf_op jit(solution)/shard_map/ppermute | solution.py:841
  283.6 20.5 %collective-permute-start.26 = (bf16[2,96,768]{2,1,0:T(8,128)(2,1)S(1)}, bf16[2,96,768]{2,1,0:T(8,128)(2,1)S(1)}, u32[]{:S(2)}, u32[]{:S(2)}) collective-permute-start(bf16[2,96,768]{2,1,0:T(8,128)(2,1)S(1)} %get-tuple-element.262.refs_0_), channel_id=1, source_target_pairs={{0,1},{1,0},{2,3},{3,2},{4,5},{5,4},{6,7},{7,6},{8,9},{9,8},{10,11... | collective-permute-start | bytes 884744 | tf_op jit(solution)/shard_map/ppermute | solution.py:841
  284.1 41.9 %collective-permute-start.30 = (bf16[4,96,768]{2,1,0:T(8,128)(2,1)S(1)}, bf16[4,96,768]{2,1,0:T(8,128)(2,1)S(1)}, u32[]{:S(2)}, u32[]{:S(2)}) collective-permute-start(bf16[4,96,768]{2,1,0:T(8,128)(2,1)S(1)} %get-tuple-element.273.refs_0_), channel_id=1, source_target_pairs={{0,2},{1,3},{2,0},{3,1},{4,6},{5,7},{6,4},{7,5},{8,10},{9,11},{10,... | collective-permute-start | bytes 1769480 | tf_op jit(solution)/shard_map/ppermute | solution.py:841
  304.2 21.6 %collective-permute-start.31 = (bf16[2,96,768]{2,1,0:T(8,128)(2,1)S(1)}, bf16[2,96,768]{2,1,0:T(8,128)(2,1)S(1)}, u32[]{:S(2)}, u32[]{:S(2)}) collective-permute-start(bf16[2,96,768]{2,1,0:T(8,128)(2,1)S(1)} %get-tuple-element.274.refs_0_), channel_id=1, source_target_pairs={{0,2},{1,3},{2,0},{3,1},{4,6},{5,7},{6,4},{7,5},{8,10},{9,11},{10,... | collective-permute-start | bytes 884744 | tf_op jit(solution)/shard_map/ppermute | solution.py:841
  (70 other events, 637.2 us)
Sparse Core Ops, SparseCore 0:
  60.7 39.0 all-gather.6
  101.6 38.9 all-gather.10
  143.0 54.7 all-gather.8
